TPU v7x, 32 devices: a whole 2x2x4 slice. The times are simulated.
32 devices in a mesh: box: 8 (over z, y), col: 4 (over x, core).
Axes of the slice: x: 2, y: 2, z: 4, core: 2. Of those that a mesh axis runs over, the one named last changes fastest.
Arguments:
- basis: float32 [4, 2, 64, 4096], P(None, None, 'col', 'box'), may hold values from -1000 to 1000
- offsets: float32 [3, 4096], P(None, 'box'), may hold values from -0.5 to 0.5
- weights: float32 [4096], P('box'), may hold values from 0.03 to 0.3
- interp: float32 [32, 32, 128], P('box'), may hold values from 0 to 1
- skeleton: int32 [32, 32], P('box'), may hold values from 0 to 127, as said below
- near_boxes: int32 [32, 27], P('box'), may hold values from 0 to 31, as said below
- near_count: int32 [32], P('box'), may hold values from 3 to 27, as said below
Outputs:
- new_block: float32 [2, 64, 4096], P(None, 'col', 'box')
- coupling: float32 [4, 64, 64], replicated
- factor: float32 [64, 64], replicated
Inputs may be any that keep to these rules, and one draw needn't show every extreme that they name: `skeleton`: each row holds 32 different points of the box. `near_boxes`: entry 0 of box b's row is b itself, entry 1 is b + 4 and entry 2 is b - 4, both clipped to the boxes; every entry lies within 4 boxes of b. Box b's near field is the first near_count[b] entries of its row of near_boxes.
All inputs are finite; a program needn't handle non-finite values.
Results may differ from a plain program's by a relative error of at most 0.0003.
Values sent between devices are 32-bit elements; how exact they have to be, the bound alone decides.
A program may use at most 64 MiB of HBM per device.

v0:
```python
import math

import jax
import jax.numpy as jnp
from jax import lax
from jax.sharding import PartitionSpec as P

BOX_DEV = 4


WAVENUMBER = 6.0
SMOOTHING = 0.1
SHIFT_SCALE = 0.02
EPSILON = 1e-06
HIGHEST = lax.Precision.HIGHEST
SOURCE_BLOCK = 2048


def extended_2(cells, sides, width):
    for axis, dim in sides:
        count = lax.axis_size(axis)
        ends = count - 1
        head = lax.slice_in_dim(cells, 0, width, axis=dim)
        tail = lax.slice_in_dim(cells, cells.shape[dim] - width, cells.shape[dim], axis=dim)
        cells = jnp.concatenate(
            [
                lax.ppermute(tail, axis, [(i, (i + 1) % count) for i in range(ends)]),
                cells,
                lax.ppermute(head, axis, [((i + 1) % count, i) for i in range(ends)]),
            ],
            axis=dim,
        )
    return cells


def box_centers(box_index):
    along_band = (box_index // BOX_DEV).astype(jnp.float32)
    across = (box_index % BOX_DEV).astype(jnp.float32)
    return jnp.stack([along_band, across, jnp.zeros_like(along_band)])


def helmholtz_pair(targets, sources):
    spread = SMOOTHING * SMOOTHING
    for axis_index in range(3):
        spread = (
            spread + (targets[axis_index][..., :, None] - sources[axis_index][..., None, :]) ** 2
        )
    distance = jnp.sqrt(spread)
    factor = 1.0 / (4.0 * math.pi * distance)
    return (jnp.cos(WAVENUMBER * distance) * factor, jnp.sin(WAVENUMBER * distance) * factor)


def far_block(skel_count, target_pos, target_weight, running, shard_piece, first_row):
    value_rows = shard_piece.shape[0] - 3
    source_count = shard_piece.shape[1]
    source_boxes = source_count // skel_count
    target_count = target_pos.shape[1]
    box_weight = lax.dynamic_slice_in_dim(target_weight, first_row // skel_count, source_boxes, 1)
    kernel_re, kernel_im = helmholtz_pair(target_pos, shard_piece[value_rows:])
    kernel_re = (
        kernel_re.reshape(target_count, source_boxes, skel_count) * box_weight[:, :, None]
    ).reshape(target_count, source_count)
    kernel_im = (
        kernel_im.reshape(target_count, source_boxes, skel_count) * box_weight[:, :, None]
    ).reshape(target_count, source_count)
    stacked = jnp.stack([kernel_re, kernel_im])
    charge_rows = shard_piece[:value_rows].reshape(2, value_rows // 2, source_count)
    product = jnp.einsum("gts,pcs->gpct", stacked, charge_rows, precision=HIGHEST)
    return running + jnp.stack([product[0, 0] - product[1, 1], product[1, 0] + product[0, 1]])


def far_fold(skel_count, target_pos, target_weight, running, shard_piece, first_row):
    source_count = shard_piece.shape[1]
    if source_count > SOURCE_BLOCK and source_count % SOURCE_BLOCK == 0:

        def one_block(block_index, carry):
            offset = block_index * SOURCE_BLOCK
            block_piece = lax.dynamic_slice_in_dim(shard_piece, offset, SOURCE_BLOCK, 1)
            return far_block(
                skel_count, target_pos, target_weight, carry, block_piece, first_row + offset
            )

        return lax.fori_loop(0, source_count // SOURCE_BLOCK, one_block, running)
    return far_block(skel_count, target_pos, target_weight, running, shard_piece, first_row)


def shards(basis, offsets, weights, interp, skeleton, near_boxes, near_count):
    box_count = near_count.shape[0]
    points = interp.shape[2]
    skel_count = interp.shape[1]
    slot_count = near_boxes.shape[1]
    prior_blocks = basis.shape[0]
    columns = basis.shape[2]
    total_boxes = box_count * lax.axis_size("box")
    first_box = lax.axis_index("box") * box_count
    own_boxes = first_box + jnp.arange(box_count, dtype=jnp.int32)
    positions = offsets.reshape(3, box_count, points) + box_centers(own_boxes)[:, :, None]
    current = basis[prior_blocks - 1]
    sources = (current * weights).reshape(2, columns, box_count, points)
    payload = jnp.concatenate([sources.reshape(2 * columns, box_count, points), positions], axis=0)
    extended = extended_2(payload, (("box", 1),), box_count)

    def near_slot(slot_index, running):
        listed = lax.dynamic_index_in_dim(near_boxes, slot_index, 1, keepdims=False)
        live_slot = (slot_index < near_count).astype(jnp.float32)
        picked = jnp.take(extended, listed - first_box + box_count, axis=1)
        source_pos = picked[2 * columns :]
        source_val = (picked[: 2 * columns] * live_slot[None, :, None]).reshape(
            2, columns, box_count, points
        )
        kernel_re, kernel_im = helmholtz_pair(positions, source_pos)
        stacked = jnp.stack([kernel_re, kernel_im])
        product = jnp.einsum("gbtq,pcbq->gpcbt", stacked, source_val, precision=HIGHEST)
        return running + jnp.stack([product[0, 0] - product[1, 1], product[1, 0] + product[0, 1]])

    near_init = jnp.zeros((2, columns, box_count, points), jnp.float32)
    near_field = lax.fori_loop(0, slot_count, near_slot, near_init)
    charges = jnp.einsum("bkq,pcbq->pcbk", interp, sources, precision=HIGHEST).reshape(
        2, columns, box_count * skel_count
    )
    skel_pos = jnp.take_along_axis(
        positions, jnp.broadcast_to(skeleton[None], (3, box_count, skel_count)), axis=2
    ).reshape(3, box_count * skel_count)
    slot_live = jnp.arange(slot_count, dtype=jnp.int32)[None, :] < near_count[:, None]
    every_box = jnp.arange(total_boxes, dtype=jnp.int32)
    box_listed = jnp.any(
        (near_boxes[:, :, None] == every_box[None, None, :]) & slot_live[:, :, None], axis=1
    )
    target_weight = jnp.repeat(1.0 - box_listed.astype(jnp.float32), skel_count, axis=0)
    payload_far = jnp.concatenate(
        [charges.reshape(2 * columns, box_count * skel_count), skel_pos], axis=0
    )
    zero_phi = jnp.zeros((2, columns, box_count * skel_count), jnp.float32)
    potentials = far_fold(
        skel_count,
        skel_pos,
        target_weight,
        zero_phi,
        lax.all_gather(payload_far, "box", axis=1, tiled=True),
        jnp.int32(0),
    )
    potentials = potentials.reshape(2, columns, box_count, skel_count)
    far_field = jnp.einsum("bkq,pcbk->pcbq", interp, potentials, precision=HIGHEST)
    applied = 0.5 * current + (near_field + far_field).reshape(2, columns, box_count * points)
    rows_basis, rows_applied = (
        lax.all_to_all(basis, "col", split_axis=3, concat_axis=2, tiled=True),
        lax.all_to_all(applied[None], "col", split_axis=3, concat_axis=2, tiled=True),
    )
    rows_applied = rows_applied[0]
    all_columns = rows_applied.shape[1]
    row_total = rows_applied.shape[2] * lax.axis_size("box") * lax.axis_size("col")
    part_coupling = (
        jnp.einsum("kpiq,pjq->kij", rows_basis, rows_applied, precision=HIGHEST) / row_total
    )
    part_plain = (
        jnp.einsum("piq,pjq->ij", rows_applied, rows_applied, precision=HIGHEST) / row_total
    )
    part_correlation = (
        jnp.einsum("kpiq,lpjq->kilj", rows_basis, rows_basis, precision=HIGHEST) / row_total
    )
    coupling, plain_gram, correlation = lax.psum(
        (part_coupling, part_plain, part_correlation), ("box", "col")
    )
    flat_coupling = coupling.reshape(prior_blocks * all_columns, all_columns)
    cross_term = jnp.dot(flat_coupling.T, flat_coupling, precision=HIGHEST)
    flat_correlation = correlation.reshape(prior_blocks * all_columns, prior_blocks * all_columns)
    sandwich = jnp.dot(
        flat_coupling.T,
        jnp.dot(flat_correlation, flat_coupling, precision=HIGHEST),
        precision=HIGHEST,
    )
    gram_matrix = plain_gram - 2.0 * cross_term + sandwich
    residual = rows_applied - jnp.einsum("kpiq,kij->pjq", rows_basis, coupling, precision=HIGHEST)
    identity = jnp.eye(all_columns, dtype=jnp.float32)
    shift_term = SHIFT_SCALE * jnp.trace(gram_matrix) / all_columns + EPSILON
    lower_factor = jnp.linalg.cholesky(gram_matrix + shift_term * identity)
    inverse = jax.scipy.linalg.solve_triangular(lower_factor, identity, lower=True)
    normalized = jnp.einsum("ij,pjq->piq", inverse, residual, precision=HIGHEST)
    new_block = lax.all_to_all(normalized, "col", split_axis=1, concat_axis=2, tiled=True)
    return (new_block, coupling, lower_factor.T)


def solution(mesh):
    return jax.shard_map(
        shards,
        mesh=mesh,
        in_specs=(
            P(None, None, "col", "box"),
            P(None, "box"),
            P("box"),
            P("box", None, None),
            P("box", None),
            P("box", None),
            P("box"),
        ),
        out_specs=(P(None, "col", "box"), P(), P()),
        check_vma=False,
    )
```

profile of v0, /device:TPU:0, one launch (start us, length us, event | category | flops | bytes accessed | tf_op | source)
XLA Modules:
  0.0 318.2 jit_solution(2153825559556843144)
XLA Ops:
  9.7 1.3 collective-permute-start.1
  11.0 5.5 %collective-permute-start = (f32[35,4,128]{2,0,1:T(8,128)S(1)}, f32[35,4,128]{2,0,1:T(8,128)S(1)}, u32[]{:S(2)}, u32[]{:S(2)}) collective-permute-start(f32[35,4,128]{2,0,1:T(8,128)S(1)} %pad_maximum_fusion.1), channel_id=1, source_target_pairs={{0,4},{4,8},{8,12},{12,16},{16,20},{20,24},{24,28},{1,5},{5,9},{9,... | collective-permute-start | bytes 215048 | tf_op jit(solution)/shard_map/ppermute | solution.py:27
  19.7 3.8 %gather_fusion.1 = f32[384]{0:T(512)S(1)} fusion(f32[3,4,128]{2,1,0:T(4,128)S(1)} %broadcast_add_fusion, s32[384]{0:T(512)S(1)} %reshape.752), kind=kCustom, calls=%fused_computation.1 | custom fusion | bytes 7680 | tf_op jit(solution)/shard_map/jit(take_along_axis)/gather | solution.py:121
  24.0 31.5 %all_gather.3 = f32[35,1024]{1,0:T(8,128)S(1)} all-gather(f32[35,128]{1,0:T(8,128)S(1)} %pad_maximum_fusion.2), channel_id=1, replica_groups=mesh['box'=8,'col'=4] {'box'}, dimensions={1}, use_global_device_ids=true | all-gather | bytes 161280 | tf_op jit(solution)/shard_map/all_gather | solution.py:139
  56.7 2.3 multiply_multiply_fusion.1
  60.3 71.2 %while.16 = (s32[]{:T(128)}, f32[2,16,4,128]{3,1,2,0:T(8,128)S(1)}, s32[4,27]{0,1:T(8,128)S(1)}, s32[]{:T(128)}, f32[35,12,128]{2,0,1:T(8,128)S(1)}, /*index=5*/...) while((s32[]{:T(128)}, f32[2,16,4,128]{3,1,2,0:T(8,128)S(1)}, ...), condition=%wide.region_1.2_spmd.clone, body=%wide.region_0.1_spmd.clone.sunk | while | flops 51481128 | bytes 2097395 | solution.py:117
  61.1 1.2 cosine_multiply_fusion.2
  66.4 1.2 cosine_multiply_fusion.2
  132.0 1.4 reshape.778
  133.4 3.3 %all-to-all-start = ((f32[4,1,4096]{2,1,0:T(1,128)}), f32[4,1,4096]{2,1,0:T(1,128)S(1)}, u32[]{:S(2)}, u32[]{:S(2)}) async-start(f32[4,1,4096]{2,1,0:T(1,128)} %reshape.778), calls=%async_computation | async-start | bytes 131072 | tf_op jit(solution)/shard_map/all_to_all | solution.py:147
  137.8 2.3 reshape.780
  140.8 3.4 %all-to-all-start.1 = ((f32[4,1,16384]{2,1,0:T(1,128)}), f32[4,1,16384]{2,1,0:T(1,128)S(1)}, u32[]{:S(2)}, u32[]{:S(2)}) async-start(f32[4,1,16384]{2,1,0:T(1,128)} %reshape.780), calls=%async_computation.1 | async-start | bytes 524288 | tf_op jit(solution)/shard_map/all_to_all | solution.py:146
  146.6 3.6 %all-to-all-done.1 = f32[4,1,16384]{2,1,0:T(1,128)S(1)} async-done(((f32[4,1,16384]{2,1,0:T(1,128)}), f32[4,1,16384]{2,1,0:T(1,128)S(1)}, u32[]{:S(2)}, u32[]{:S(2)}) %all-to-all-start.1) | async-done | bytes 262176 | tf_op jit(solution)/shard_map/all_to_all | solution.py:146
  150.2 1.4 reduce.7
  151.6 1.5 reshape.781
  157.5 37.2 %psum.22 = f32[64,64]{1,0:T(8,128)S(1)} all-reduce(f32[64,64]{1,0:T(8,128)S(1)} %fusion.13), channel_id=1, replica_groups=mesh['box'=8,'col'=4] {'box','col'}, use_global_device_ids=true, to_apply=%region_4.5 | all-reduce | flops 4096 | bytes 32768 | tf_op jit(solution)/shard_map/psum | solution.py:161
  195.7 87.8 %all-reduce.3.cloned.1.call-done = (f32[4,64,64]{1,2,0:T(8,128)}, f32[256,256]{1,0:T(8,128)}) async-done(((f32[4,64,64]{1,2,0:T(8,128)}, f32[256,256]{1,0:T(8,128)}), (f32[4,64,64]{1,2,0:T(8,128)}, f32[256,256]{1,0:T(8,128)})) %all-reduce.3.cloned.1.call-update) | async-done | bytes 327696 | tf_op jit(solution)/shard_map/psum | solution.py:161
  284.6 1.2 fusion.10
  285.8 1.2 fusion.12
  287.2 1.3 fusion.38
  290.1 5.8 %cholesky.18 = f32[64,64]{1,0:T(8,128)S(1)} custom-call(f32[64,64]{1,0:T(8,128)S(1)} %fusion.25), custom_call_target="Cholesky" | custom-call | tf_op jit(solution)/shard_map/jit(cholesky)/cholesky | solution.py:176
  297.2 4.9 %custom-call.7 = f32[1,64,64]{1,2,0:T(8,128)S(1)} custom-call(f32[1,64,64]{2,1,0:T(8,128)S(1)} %get-tuple-element.286), custom_call_target="InvertDiagBlocksLowerTriangular" | custom-call | tf_op jit(solution)/shard_map/jit(_solve_triangular)/triangular_solve | solution.py:177
  303.3 3.3 %all-to-all-start.2 = ((f32[2,64,128]{2,0,1:T(2,128)}), f32[2,64,128]{2,0,1:T(2,128)S(1)}, u32[]{:S(2)}, u32[]{:S(2)}) async-start(f32[2,64,128]{2,0,1:T(2,128)} %copy.123), calls=%async_computation.2 | async-start | bytes 131072 | tf_op jit(solution)/shard_map/all_to_all | solution.py:179
  308.0 2.6 all-to-all-done.2
  (449 shorter events, 91.5 us)
Async XLA Ops:
  7.2 16.4 %copy-start = (f32[4,32,128]{2,1,0:T(8,128)S(1)}, f32[4,32,128]{2,1,0:T(8,128)}, u32[]{:S(2)}) copy-start(f32[4,32,128]{2,1,0:T(8,128)} %param.12) | copy-start | bytes 196612
  9.7 50.5 %collective-permute-start.1 = (f32[35,4,128]{2,0,1:T(8,128)S(1)}, f32[35,4,128]{2,0,1:T(8,128)S(1)}, u32[]{:S(2)}, u32[]{:S(2)}) collective-permute-start(f32[35,4,128]{2,0,1:T(8,128)S(1)} %pad_maximum_fusion.1), channel_id=1, source_target_pairs={{4,0},{8,4},{12,8},{16,12},{20,16},{24,20},{28,24},{5,1},{9,5},{13... | collective-permute-start | bytes 215048 | tf_op jit(solution)/shard_map/ppermute | solution.py:29
  11.0 49.2 %collective-permute-start = (f32[35,4,128]{2,0,1:T(8,128)S(1)}, f32[35,4,128]{2,0,1:T(8,128)S(1)}, u32[]{:S(2)}, u32[]{:S(2)}) collective-permute-start(f32[35,4,128]{2,0,1:T(8,128)S(1)} %pad_maximum_fusion.1), channel_id=1, source_target_pairs={{0,4},{4,8},{8,12},{12,16},{16,20},{20,24},{24,28},{1,5},{5,9},{9,... | collective-permute-start | bytes 215048 | tf_op jit(solution)/shard_map/ppermute | solution.py:27
  19.7 3.9 %copy-start.4 = (f32[512]{0:T(512)S(1)}, f32[512]{0:T(512)}, u32[]{:S(2)}) copy-start(f32[512]{0:T(512)} %param.11) | copy-start | bytes 6148
  19.7 35.9 %copy-start.5 = (s32[4,27]{1,0:T(4,128)S(1)}, s32[4,27]{1,0:T(4,128)}, u32[]{:S(2)}) copy-start(s32[4,27]{1,0:T(4,128)} %param.14) | copy-start | bytes 1300
  19.7 36.0 %copy-start.6 = (s32[4]{0:T(128)S(1)}, s32[4]{0:T(128)}, u32[]{:S(2)}) copy-start(s32[4]{0:T(128)} %param.15) | copy-start | bytes 52
  23.5 32.8 %copy-start.3 = (s32[4,32]{1,0:T(4,128)S(1)}, s32[4,32]{1,0:T(4,128)}, u32[]{:S(2)}) copy-start(s32[4,32]{1,0:T(4,128)} %param.13) | copy-start | bytes 1540
  60.3 71.5 %copy-start.2 = (f32[4,2,16,512]{3,2,1,0:T(8,128)S(1)}, f32[4,2,16,512]{3,2,1,0:T(8,128)}, u32[]{:S(2)}) copy-start(f32[4,2,16,512]{3,2,1,0:T(8,128)} %param.9) | copy-start | bytes 786436
  133.4 7.4 %all-to-all-start = ((f32[4,1,4096]{2,1,0:T(1,128)}), f32[4,1,4096]{2,1,0:T(1,128)S(1)}, u32[]{:S(2)}, u32[]{:S(2)}) async-start(f32[4,1,4096]{2,1,0:T(1,128)} %reshape.778), calls=%async_computation | async-start | bytes 131072 | tf_op jit(solution)/shard_map/all_to_all | solution.py:147
  140.8 9.4 %all-to-all-start.1 = ((f32[4,1,16384]{2,1,0:T(1,128)}), f32[4,1,16384]{2,1,0:T(1,128)S(1)}, u32[]{:S(2)}, u32[]{:S(2)}) async-start(f32[4,1,16384]{2,1,0:T(1,128)} %reshape.780), calls=%async_computation.1 | async-start | bytes 524288 | tf_op jit(solution)/shard_map/all_to_all | solution.py:146
  144.2 139.3 %all-reduce.3.cloned.1.call-start = ((), (), s32[]{:S(2)}) async-start(), calls=%async_computation.3 | async-start | bytes 786432 | tf_op jit(solution)/shard_map/psum | solution.py:161
  283.5 23.1 %copy-start.1 = (f32[4,64,64]{1,2,0:T(8,128)S(1)}, f32[4,64,64]{1,2,0:T(8,128)}, u32[]{:S(2)}) copy-start(f32[4,64,64]{1,2,0:T(8,128)} %get-tuple-element.268) | copy-start | bytes 196612
  303.3 7.4 %all-to-all-start.2 = ((f32[2,64,128]{2,0,1:T(2,128)}), f32[2,64,128]{2,0,1:T(2,128)S(1)}, u32[]{:S(2)}, u32[]{:S(2)}) async-start(f32[2,64,128]{2,0,1:T(2,128)} %copy.123), calls=%async_computation.2 | async-start | bytes 131072 | tf_op jit(solution)/shard_map/all_to_all | solution.py:179
Sparse Core Ops, SparseCore 0:
  157.4 126.0 all-reduce.2
where the time goes:
time: 319 us; the launch traced here: 318 us
  waiting for transfers between devices  94.8 us (30%)
  blocking collectives  68.7 us (22%)
  other arithmetic  57.2 us (18%)
  local copies, waits for them, and re-layouts  38.4 us (12%)
  matrix products  24.5 us (8%)
  starting transfers between devices  17 us (5%)
  between operations  15.2 us (5%)
    psum x1, waiting for transfers between devices, shards(): lax.psum((part_coupling, part_plain, part_correlation), ('box', 'col'))  87.8 us
    psum x1, blocking collectives, shards(): lax.psum((part_coupling, part_plain, part_correlation), ('box', 'col'))  37.2 us
    mul x27, other arithmetic, helmholtz_pair(): jnp.cos(WAVENUMBER * distance) * factor  31.7 us
    all_gather x1, blocking collectives, shards(): lax.all_gather(payload_far, 'box', axis=1, tiled=True)  31.5 us
    dot_general x27, matrix products, near_slot(): jnp.einsum('gbtq,pcbq->gpcbt', stacked, source_val, precision=HIGHEST)  16 us
    gather x27, local copies, waits for them, and re-layouts, near_slot(): picked = jnp.take(extended, listed - first_box + box_count, axis=1)  15 us
    unnamed x22, local copies, waits for them, and re-layouts  8.47 us
    another operation x3, other arithmetic, shards(): lower_factor = jnp.linalg.cholesky(gram_matrix + shift_term * identity)  6.52 us
  transfers between devices with their start and end apart: 6, of which 4 were waited for; matrix products, arithmetic and copies ran while one was open for 6% of the time, Pallas kernels for 0%

commit v1 on v0

--- a/solution.py
+++ b/solution.py
@@ -84,6 +84,20 @@
     return far_block(skel_count, target_pos, target_weight, running, shard_piece, first_row)
 
 
+def gather_by_exchange(piece, axes, count):
+    return lax.all_to_all(
+        jnp.broadcast_to(piece[None], (count,) + piece.shape), axes, split_axis=0, concat_axis=0
+    )
+
+
+def sum_by_exchange(partial, axes, count):
+    rows = partial.shape[0] // count
+    pieces = lax.all_to_all(
+        partial.reshape((count, rows) + partial.shape[1:]), axes, split_axis=0, concat_axis=0
+    )
+    return gather_by_exchange(jnp.sum(pieces, axis=0), axes, count).reshape(partial.shape)
+
+
 def shards(basis, offsets, weights, interp, skeleton, near_boxes, near_count):
     box_count = near_count.shape[0]
     points = interp.shape[2]
@@ -91,86 +105,73 @@
     slot_count = near_boxes.shape[1]
     prior_blocks = basis.shape[0]
     columns = basis.shape[2]
-    total_boxes = box_count * lax.axis_size("box")
+    box_size = lax.axis_size("box")
+    total_boxes = box_count * box_size
+    devices = box_size * lax.axis_size("col")
     first_box = lax.axis_index("box") * box_count
     own_boxes = first_box + jnp.arange(box_count, dtype=jnp.int32)
     positions = offsets.reshape(3, box_count, points) + box_centers(own_boxes)[:, :, None]
+    rows_basis = lax.all_to_all(basis, "col", split_axis=3, concat_axis=2, tiled=True)
     current = basis[prior_blocks - 1]
     sources = (current * weights).reshape(2, columns, box_count, points)
     payload = jnp.concatenate([sources.reshape(2 * columns, box_count, points), positions], axis=0)
     extended = extended_2(payload, (("box", 1),), box_count)
-
-    def near_slot(slot_index, running):
-        listed = lax.dynamic_index_in_dim(near_boxes, slot_index, 1, keepdims=False)
-        live_slot = (slot_index < near_count).astype(jnp.float32)
-        picked = jnp.take(extended, listed - first_box + box_count, axis=1)
-        source_pos = picked[2 * columns :]
-        source_val = (picked[: 2 * columns] * live_slot[None, :, None]).reshape(
-            2, columns, box_count, points
-        )
-        kernel_re, kernel_im = helmholtz_pair(positions, source_pos)
-        stacked = jnp.stack([kernel_re, kernel_im])
-        product = jnp.einsum("gbtq,pcbq->gpcbt", stacked, source_val, precision=HIGHEST)
-        return running + jnp.stack([product[0, 0] - product[1, 1], product[1, 0] + product[0, 1]])
-
-    near_init = jnp.zeros((2, columns, box_count, points), jnp.float32)
-    near_field = lax.fori_loop(0, slot_count, near_slot, near_init)
     charges = jnp.einsum("bkq,pcbq->pcbk", interp, sources, precision=HIGHEST).reshape(
         2, columns, box_count * skel_count
     )
-    skel_pos = jnp.take_along_axis(
-        positions, jnp.broadcast_to(skeleton[None], (3, box_count, skel_count)), axis=2
-    ).reshape(3, box_count * skel_count)
+    hot = (skeleton[:, :, None] == jnp.arange(points, dtype=jnp.int32)).astype(jnp.float32)
+    skel_pos = jnp.einsum("bkq,dbq->dbk", hot, positions, precision=HIGHEST).reshape(
+        3, box_count * skel_count
+    )
     slot_live = jnp.arange(slot_count, dtype=jnp.int32)[None, :] < near_count[:, None]
+    payload_far = jnp.concatenate(
+        [charges.reshape(2 * columns, box_count * skel_count), skel_pos], axis=0
+    )
+    gathered = gather_by_exchange(payload_far, "box", box_size)
+    gathered = jnp.moveaxis(gathered, 0, 1).reshape(payload_far.shape[0], -1)
+    reach = box_count
+    window = 2 * reach + 1
+    shift_index = jnp.arange(window, dtype=jnp.int32) - reach
+    listed = near_boxes[:, :, None] == (own_boxes[:, None] + shift_index[None, :])[:, None, :]
+    times = jnp.sum((listed & slot_live[:, :, None]).astype(jnp.float32), axis=1)
+    windows = jnp.stack([extended[:, i : i + window] for i in range(box_count)], axis=1)
+    source_pos = windows[2 * columns :].reshape(3, box_count, window * points)
+    source_val = (windows[: 2 * columns] * times[None, :, :, None]).reshape(
+        2, columns, box_count, window * points
+    )
+    kernel_re, kernel_im = helmholtz_pair(positions, source_pos)
+    stacked = jnp.stack([kernel_re, kernel_im])
+    product = jnp.einsum("gbtq,pcbq->gpcbt", stacked, source_val, precision=HIGHEST)
+    near_field = jnp.stack([product[0, 0] - product[1, 1], product[1, 0] + product[0, 1]])
     every_box = jnp.arange(total_boxes, dtype=jnp.int32)
     box_listed = jnp.any(
         (near_boxes[:, :, None] == every_box[None, None, :]) & slot_live[:, :, None], axis=1
     )
     target_weight = jnp.repeat(1.0 - box_listed.astype(jnp.float32), skel_count, axis=0)
-    payload_far = jnp.concatenate(
-        [charges.reshape(2 * columns, box_count * skel_count), skel_pos], axis=0
-    )
     zero_phi = jnp.zeros((2, columns, box_count * skel_count), jnp.float32)
     potentials = far_fold(
-        skel_count,
-        skel_pos,
-        target_weight,
-        zero_phi,
-        lax.all_gather(payload_far, "box", axis=1, tiled=True),
-        jnp.int32(0),
+        skel_count, skel_pos, target_weight, zero_phi, gathered, jnp.int32(0)
     )
     potentials = potentials.reshape(2, columns, box_count, skel_count)
     far_field = jnp.einsum("bkq,pcbk->pcbq", interp, potentials, precision=HIGHEST)
     applied = 0.5 * current + (near_field + far_field).reshape(2, columns, box_count * points)
-    rows_basis, rows_applied = (
-        lax.all_to_all(basis, "col", split_axis=3, concat_axis=2, tiled=True),
-        lax.all_to_all(applied[None], "col", split_axis=3, concat_axis=2, tiled=True),
-    )
-    rows_applied = rows_applied[0]
+    rows_applied = lax.all_to_all(applied, "col", split_axis=2, concat_axis=1, tiled=True)
     all_columns = rows_applied.shape[1]
-    row_total = rows_applied.shape[2] * lax.axis_size("box") * lax.axis_size("col")
+    row_total = rows_applied.shape[2] * devices
     part_coupling = (
         jnp.einsum("kpiq,pjq->kij", rows_basis, rows_applied, precision=HIGHEST) / row_total
+    ).reshape(prior_blocks * all_columns, all_columns)
+
+    def total(partial):
+        if partial.shape[0] % devices == 0 and devices <= 64:
+            return sum_by_exchange(partial, ("box", "col"), devices)
+        return lax.psum(partial, ("box", "col"))
+
+    coupling = total(part_coupling).reshape(prior_blocks, all_columns, all_columns)
+    residual = rows_applied - jnp.einsum("kpiq,kij->pjq", rows_basis, coupling, precision=HIGHEST)
+    gram_matrix = total(
+        jnp.einsum("piq,pjq->ij", residual, residual, precision=HIGHEST) / row_total
     )
-    part_plain = (
-        jnp.einsum("piq,pjq->ij", rows_applied, rows_applied, precision=HIGHEST) / row_total
-    )
-    part_correlation = (
-        jnp.einsum("kpiq,lpjq->kilj", rows_basis, rows_basis, precision=HIGHEST) / row_total
-    )
-    coupling, plain_gram, correlation = lax.psum(
-        (part_coupling, part_plain, part_correlation), ("box", "col")
-    )
-    flat_coupling = coupling.reshape(prior_blocks * all_columns, all_columns)
-    cross_term = jnp.dot(flat_coupling.T, flat_coupling, precision=HIGHEST)
-    flat_correlation = correlation.reshape(prior_blocks * all_columns, prior_blocks * all_columns)
-    sandwich = jnp.dot(
-        flat_coupling.T,
-        jnp.dot(flat_correlation, flat_coupling, precision=HIGHEST),
-        precision=HIGHEST,
-    )
-    gram_matrix = plain_gram - 2.0 * cross_term + sandwich
-    residual = rows_applied - jnp.einsum("kpiq,kij->pjq", rows_basis, coupling, precision=HIGHEST)
     identity = jnp.eye(all_columns, dtype=jnp.float32)
     shift_term = SHIFT_SCALE * jnp.trace(gram_matrix) / all_columns + EPSILON
     lower_factor = jnp.linalg.cholesky(gram_matrix + shift_term * identity)

time: 319 us -> 133 us (0.42)
  waiting for transfers between devices: 94.8 us -> 16.7 us
  blocking collectives: 68.7 us -> 22.6 us
  other arithmetic: 57.2 us -> 33.5 us
  local copies, waits for them, and re-layouts: 38.4 us -> 20 us
  matrix products: 24.5 us -> 8.99 us
  between operations: 15.2 us -> 1.85 us
  starting transfers between devices: 17 us -> 28.5 us
    psum x1 -> x0, waiting for transfers between devices: 87.8 us -> none  [shards(): lax.psum((part_coupling, part_plain, part_correlation), ('box', 'col'))]
    psum x1 -> x0, blocking collectives: 37.2 us -> none  [shards(): lax.psum((part_coupling, part_plain, part_correlation), ('box', 'col'))]
    all_gather x1 -> x0, blocking collectives: 31.5 us -> none  [shards(): lax.all_gather(payload_far, 'box', axis=1, tiled=True)]
    all_to_all x0 -> x2, blocking collectives: none -> 22.6 us  [sum_by_exchange(): lax.all_to_all(partial.reshape((count, rows) + partial.shape[1:]), axes,...]
    mul x27 -> x1, other arithmetic: 31.7 us -> 10.1 us  [helmholtz_pair(): jnp.cos(WAVENUMBER * distance) * factor]
    gather x30 -> x0, local copies, waits for them, and re-layouts: 19 us -> none  [the longest x27 15 us: near_slot(): picked = jnp.take(extended, listed - first_box + box_count, axis=1)]
    dot_general x32 -> x3, matrix products: 20.2 us -> 5.55 us  [the longest x1 4.45 us: shards(): jnp.einsum('gbtq,pcbq->gpcbt', stacked, source_val, precision=HIGHEST)]
    all_to_all x1 -> x4, waiting for transfers between devices: 0.76 us -> 13.3 us  [the longest x3 13.3 us: gather_by_exchange(): lax.all_to_all(jnp.broadcast_to(piece[None], (count,) + piece.shape), axe...]
  transfers between devices with their start and end apart: 6 -> 8, of which waited for: 4 -> 3; matrix products, arithmetic and copies ran while one was open for 6% -> 28% of each run, Pallas kernels for 0% -> 0%
where the time goes in v1:
time: 133 us; the launch traced here: 132 us
  other arithmetic  33.5 us (25%)
  starting transfers between devices  28.5 us (21%)
  blocking collectives  22.6 us (17%)
  local copies, waits for them, and re-layouts  20 us (15%)
  waiting for transfers between devices  16.7 us (13%)
  matrix products  8.99 us (7%)
  between operations  1.85 us (1%)
    all_to_all x2, blocking collectives, sum_by_exchange(): lax.all_to_all(partial.reshape((count, rows) + partial.shape[1:]), axes,...  22.6 us
    all_to_all x3, waiting for transfers between devices, gather_by_exchange(): lax.all_to_all(jnp.broadcast_to(piece[None], (count,) + piece.shape), axe...  13.3 us
    unnamed x27, local copies, waits for them, and re-layouts  11.3 us
    all_to_all x3, starting transfers between devices, gather_by_exchange(): lax.all_to_all(jnp.broadcast_to(piece[None], (count,) + piece.shape), axe...  10.9 us
    mul x1, other arithmetic, helmholtz_pair(): jnp.cos(WAVENUMBER * distance) * factor  10.1 us
    another operation x3, other arithmetic, shards(): lower_factor = jnp.linalg.cholesky(gram_matrix + shift_term * identity)  6.52 us
    ppermute x1, starting transfers between devices, extended_2(): lax.ppermute(tail, axis, [(i, (i + 1) % count) for i in range(ends)])  6.13 us
    another operation x1, other arithmetic, shards(): jax.scipy.linalg.solve_triangular(lower_factor, identity, lower=True)  4.9 us
  transfers between devices with their start and end apart: 8, of which 3 were waited for; matrix products, arithmetic and copies ran while one was open for 28% of the time, Pallas kernels for 0%

profile of v1, /device:TPU:0, one launch (start us, length us, event | category | flops | bytes accessed | tf_op | source)
XLA Modules:
  0.0 132.1 jit_solution(15186298547065222613)
XLA Ops:
  3.2 1.3 collective-permute-start.1
  4.5 6.1 %collective-permute-start = (f32[35,4,128]{2,1,0:T(4,128)S(1)}, f32[35,4,128]{2,1,0:T(4,128)}, u32[]{:S(2)}, u32[]{:S(2)}) collective-permute-start(f32[35,4,128]{2,1,0:T(4,128)S(1)} %pad_maximum_fusion.2), channel_id=1, source_target_pairs={{0,4},{4,8},{8,12},{12,16},{16,20},{20,24},{24,28},{1,5},{5,9},{9,... | collective-permute-start | bytes 215048 | tf_op jit(solution)/shard_map/ppermute | solution.py:27
  13.4 5.6 %all-to-all-start = ((f32[8,35,128]{2,1,0:T(8,128)}), f32[8,35,128]{2,1,0:T(8,128)S(1)}, u32[]{:S(2)}, u32[]{:S(2)}) async-start(f32[8,35,128]{2,1,0:T(8,128)} %broadcast_in_dim.12), calls=%async_computation | async-start | bytes 327680 | tf_op jit(solution)/shard_map/all_to_all | solution.py:88
  19.1 1.9 %copy.125 = f32[4,2,16,512]{2,0,1,3:T(4,128)S(1)} copy(f32[4,2,16,512]{3,2,1,0:T(8,128)} %param.7) | data formatting | bytes 524288 | tf_op args[0]
  22.5 2.3 %reshape.787 = f32[4,1,16384]{2,1,0:T(1,128)} reshape(f32[512,2,4,16]{3,2,1,0:T(4,128)S(1)} %bitcast.186) | data formatting | bytes 524288
  26.5 10.1 %cosine_multiply_fusion = (f32[1,4,128,1152]{3,2,0,1:T(8,128)S(1)}, f32[1,4,128,1152]{3,2,0,1:T(8,128)S(1)}) fusion(f32[4,1152]{1,0:T(4,128)S(1)} %bitcast.208, f32[4,128]{1,0:T(4,128)S(1)} %get-tuple-element.40, f32[4,1152]{1,0:T(4,128)S(1)} %bitcast.209, f32[4,128]{1,0:T(4,128)S(1)} %get-tuple-element.41, f32[4,1152]{1,0:T(4,128)S(1)} %bitcast.207, ...), kind=kLoop, calls=%fused_computation.6 | loop fusion | flops 8257536 | bytes 4780032 | tf_op jit(solution)/shard_map/mul | solution.py:50
  36.6 4.4 %fusion.3 = f32[2,2,16,4,128]{4,2,0,1,3:T(8,128)S(1)} fusion(f32[1,4,128,1152]{3,2,0,1:T(8,128)S(1)} %get-tuple-element.34, f32[1,4,128,1152]{3,2,0,1:T(8,128)S(1)} %get-tuple-element.33, f32[2,16,4,1152,1]{3,2,1,0,4:T(4,128)S(1)} %bitcast.187), kind=kOutput, calls=%fused_computation.9 | convolution fusion | flops 454164480 | bytes 5439488 | tf_op jit(solution)/shard_map/gbtq,pcbq->gpcbt/dot_general | solution.py:144
  41.0 3.6 %all-to-all-start.2 = ((f32[4,1,16384]{2,1,0:T(1,128)}), f32[4,1,16384]{2,1,0:T(1,128)S(1)}, u32[]{:S(2)}, u32[]{:S(2)}) async-start(f32[4,1,16384]{2,1,0:T(1,128)} %reshape.787), calls=%async_computation.2 | async-start | bytes 524288 | tf_op jit(solution)/shard_map/all_to_all | solution.py:114
  44.8 2.3 %multiply_multiply_fusion.1 = (f32[1,128,1024]{2,1,0:T(8,128)S(1)}, f32[1,128,1024]{2,1,0:T(8,128)S(1)}) fusion(f32[1,128,1024]{2,1,0:T(8,128)S(1)} %copy.118, f32[1024]{0:T(1024)S(1)} %bitcast.211, f32[128]{0:T(128)S(1)} %sub.248, f32[1024]{0:T(1024)S(1)} %bitcast.212, f32[128]{0:T(128)S(1)} %sub.243, f32[1024]{0:T(1024)S(1)} %bitcast.210, f32[128]{0:T(128)S(1)} %sub.238), kind=kLoop, calls=%fused_computation.31 | loop fusion | flops 2097152 | bytes 1586688 | tf_op jit(solution)/shard_map/mul | solution.py:61
  47.2 1.0 convolution_bitcast_fusion.7
  49.7 1.4 %reshape.785 = f32[4,1,4096]{2,1,0:T(1,128)} reshape(f32[512,2,16]{2,1,0:T(2,128)S(1)} %bitcast.188) | data formatting | bytes 131072
  51.1 3.3 %all-to-all-start.1 = ((f32[4,1,4096]{2,1,0:T(1,128)}), f32[4,1,4096]{2,1,0:T(1,128)S(1)}, u32[]{:S(2)}, u32[]{:S(2)}) async-start(f32[4,1,4096]{2,1,0:T(1,128)} %reshape.785), calls=%async_computation.1 | async-start | bytes 131072 | tf_op jit(solution)/shard_map/all_to_all | solution.py:158
  54.9 1.4 %reduce.20 = f32[4,16384]{1,0:T(4,128)S(1)} reduce(f32[4,1,16384]{2,1,0:T(1,128)S(1)} %all-to-all-done.2, f32[]{:T(128)} %broadcast.639), dimensions={1}, to_apply=%all_to_all.59.reduce_sub_computation | reduce | bytes 524292 | tf_op jit(solution)/shard_map/all_to_all | solution.py:114
  56.4 1.5 %reshape.788 = f32[512,2,4,16]{3,2,1,0:T(4,128)S(1)} reshape(f32[4,16384]{1,0:T(4,128)S(1)} %reduce.20) | data formatting | bytes 524288
  61.4 13.7 %all_to_all.79 = f32[32,1,512]{2,1,0:T(1,128)S(1)} all-to-all(f32[32,1,512]{2,1,0:T(1,128)S(1)} %reshape.789), channel_id=1, replica_groups=mesh['box'=8,'col'=4] {'box','col'}, dimensions={0} | all-to-all | bytes 131072 | tf_op jit(solution)/shard_map/all_to_all | solution.py:95
  76.8 2.6 %all-to-all-start.4 = ((f32[32,1,512]{2,1,0:T(1,128)}), f32[32,1,512]{2,1,0:T(1,128)S(1)}, u32[]{:S(2)}, u32[]{:S(2)}) async-start(f32[32,1,512]{2,1,0:T(1,128)} %reshape.791), calls=%async_computation.4 | async-start | bytes 131072 | tf_op jit(solution)/shard_map/all_to_all | solution.py:88
  80.4 6.4 %all-to-all-done.4 = f32[32,1,512]{2,1,0:T(1,128)S(1)} async-done(((f32[32,1,512]{2,1,0:T(1,128)}), f32[32,1,512]{2,1,0:T(1,128)S(1)}, u32[]{:S(2)}, u32[]{:S(2)}) %all-to-all-start.4) | async-done | bytes 65568 | tf_op jit(solution)/shard_map/all_to_all | solution.py:88
  88.4 8.8 %all_to_all.80 = f32[32,1,128]{2,1,0:T(1,128)S(1)} all-to-all(f32[32,1,128]{2,1,0:T(1,128)S(1)} %reshape.793), channel_id=1, replica_groups=mesh['box'=8,'col'=4] {'box','col'}, dimensions={0} | all-to-all | bytes 32768 | tf_op jit(solution)/shard_map/all_to_all | solution.py:95
  98.9 2.8 %all-to-all-start.6 = ((f32[32,1,128]{2,1,0:T(1,128)}), f32[32,1,128]{2,1,0:T(1,128)S(1)}, u32[]{:S(2)}, u32[]{:S(2)}) async-start(f32[32,1,128]{2,1,0:T(1,128)} %reshape.795), calls=%async_computation.6 | async-start | bytes 32768 | tf_op jit(solution)/shard_map/all_to_all | solution.py:88
  101.7 6.8 %all-to-all-done.6 = f32[32,1,128]{2,1,0:T(1,128)S(1)} async-done(((f32[32,1,128]{2,1,0:T(1,128)}), f32[32,1,128]{2,1,0:T(1,128)S(1)}, u32[]{:S(2)}, u32[]{:S(2)}) %all-to-all-start.6) | async-done | bytes 16416 | tf_op jit(solution)/shard_map/all_to_all | solution.py:88
  110.8 5.8 %cholesky.17 = f32[64,64]{1,0:T(8,128)S(1)} custom-call(f32[64,64]{1,0:T(8,128)S(1)} %fusion.26), custom_call_target="Cholesky" | custom-call | tf_op jit(solution)/shard_map/jit(cholesky)/cholesky | solution.py:177
  118.0 4.9 %custom-call.7 = f32[1,64,64]{1,2,0:T(8,128)S(1)} custom-call(f32[1,64,64]{2,1,0:T(8,128)S(1)} %get-tuple-element.36), custom_call_target="InvertDiagBlocksLowerTriangular" | custom-call | tf_op jit(solution)/shard_map/jit(_solve_triangular)/triangular_solve | solution.py:178
  124.0 3.3 %all-to-all-start.7 = ((f32[2,64,128]{2,0,1:T(2,128)}), f32[2,64,128]{2,0,1:T(2,128)S(1)}, u32[]{:S(2)}, u32[]{:S(2)}) async-start(f32[2,64,128]{2,0,1:T(2,128)} %copy.131), calls=%async_computation.7 | async-start | bytes 131072 | tf_op jit(solution)/shard_map/all_to_all | solution.py:180
  128.0 3.4 %all-to-all-done.7 = f32[2,64,128]{2,0,1:T(2,128)S(1)} async-done(((f32[2,64,128]{2,0,1:T(2,128)}), f32[2,64,128]{2,0,1:T(2,128)S(1)}, u32[]{:S(2)}, u32[]{:S(2)}) %all-to-all-start.7) | async-done | bytes 65568 | tf_op jit(solution)/shard_map/all_to_all | solution.py:180
  (115 shorter events, 25.4 us)
Async XLA Ops:
  0.6 11.0 %copy-start = (f32[4,32,128]{2,1,0:T(8,128)S(1)}, f32[4,32,128]{2,1,0:T(8,128)}, u32[]{:S(2)}) copy-start(f32[4,32,128]{2,1,0:T(8,128)} %param.10) | copy-start | bytes 196612
  0.6 20.4 %copy-start.3 = (s32[4]{0:T(128)S(1)}, s32[4]{0:T(128)}, u32[]{:S(2)}) copy-start(s32[4]{0:T(128)} %param.13) | copy-start | bytes 52
  0.7 20.5 %copy-start.2 = (s32[4,27]{1,0:T(4,128)S(1)}, s32[4,27]{1,0:T(4,128)}, u32[]{:S(2)}) copy-start(s32[4,27]{1,0:T(4,128)} %param.12) | copy-start | bytes 1300
  3.2 21.6 %collective-permute-start.1 = (f32[35,4,128]{2,1,0:T(4,128)S(1)}, f32[35,4,128]{2,1,0:T(4,128)}, u32[]{:S(2)}, u32[]{:S(2)}) collective-permute-start(f32[35,4,128]{2,1,0:T(4,128)S(1)} %pad_maximum_fusion.2), channel_id=1, source_target_pairs={{4,0},{8,4},{12,8},{16,12},{20,16},{24,20},{28,24},{5,1},{9,5},{13... | collective-permute-start | bytes 215048 | tf_op jit(solution)/shard_map/ppermute | solution.py:29
  4.5 20.3 %collective-permute-start = (f32[35,4,128]{2,1,0:T(4,128)S(1)}, f32[35,4,128]{2,1,0:T(4,128)}, u32[]{:S(2)}, u32[]{:S(2)}) collective-permute-start(f32[35,4,128]{2,1,0:T(4,128)S(1)} %pad_maximum_fusion.2), channel_id=1, source_target_pairs={{0,4},{4,8},{8,12},{12,16},{16,20},{20,24},{24,28},{1,5},{5,9},{9,... | collective-permute-start | bytes 215048 | tf_op jit(solution)/shard_map/ppermute | solution.py:27
  13.4 27.6 %all-to-all-start = ((f32[8,35,128]{2,1,0:T(8,128)}), f32[8,35,128]{2,1,0:T(8,128)S(1)}, u32[]{:S(2)}, u32[]{:S(2)}) async-start(f32[8,35,128]{2,1,0:T(8,128)} %broadcast_in_dim.12), calls=%async_computation | async-start | bytes 327680 | tf_op jit(solution)/shard_map/all_to_all | solution.py:88
  41.0 10.0 %all-to-all-start.2 = ((f32[4,1,16384]{2,1,0:T(1,128)}), f32[4,1,16384]{2,1,0:T(1,128)S(1)}, u32[]{:S(2)}, u32[]{:S(2)}) async-start(f32[4,1,16384]{2,1,0:T(1,128)} %reshape.787), calls=%async_computation.2 | async-start | bytes 524288 | tf_op jit(solution)/shard_map/all_to_all | solution.py:114
  51.1 7.8 %all-to-all-start.1 = ((f32[4,1,4096]{2,1,0:T(1,128)}), f32[4,1,4096]{2,1,0:T(1,128)S(1)}, u32[]{:S(2)}, u32[]{:S(2)}) async-start(f32[4,1,4096]{2,1,0:T(1,128)} %reshape.785), calls=%async_computation.1 | async-start | bytes 131072 | tf_op jit(solution)/shard_map/all_to_all | solution.py:158
  76.8 10.0 %all-to-all-start.4 = ((f32[32,1,512]{2,1,0:T(1,128)}), f32[32,1,512]{2,1,0:T(1,128)S(1)}, u32[]{:S(2)}, u32[]{:S(2)}) async-start(f32[32,1,512]{2,1,0:T(1,128)} %reshape.791), calls=%async_computation.4 | async-start | bytes 131072 | tf_op jit(solution)/shard_map/all_to_all | solution.py:88
  87.7 44.4 %copy-start.1 = (f32[32,8,64]{2,1,0:T(8,128)}, f32[32,8,64]{2,1,0:T(8,128)S(1)}, u32[]{:S(2)}) copy-start(f32[32,8,64]{2,1,0:T(8,128)S(1)} %reshape.792) | copy-start | bytes 196612
  98.9 9.6 %all-to-all-start.6 = ((f32[32,1,128]{2,1,0:T(1,128)}), f32[32,1,128]{2,1,0:T(1,128)S(1)}, u32[]{:S(2)}, u32[]{:S(2)}) async-start(f32[32,1,128]{2,1,0:T(1,128)} %reshape.795), calls=%async_computation.6 | async-start | bytes 32768 | tf_op jit(solution)/shard_map/all_to_all | solution.py:88
  124.0 7.4 %all-to-all-start.7 = ((f32[2,64,128]{2,0,1:T(2,128)}), f32[2,64,128]{2,0,1:T(2,128)S(1)}, u32[]{:S(2)}, u32[]{:S(2)}) async-start(f32[2,64,128]{2,0,1:T(2,128)} %copy.131), calls=%async_computation.7 | async-start | bytes 131072 | tf_op jit(solution)/shard_map/all_to_all | solution.py:180

commit v2 on v1

--- a/solution.py
+++ b/solution.py
@@ -1,8 +1,11 @@
+import functools
 import math
 
 import jax
 import jax.numpy as jnp
 from jax import lax
+from jax.experimental import pallas as pl
+from jax.experimental.pallas import tpu as pltpu
 from jax.sharding import PartitionSpec as P
 
 BOX_DEV = 4
@@ -90,12 +93,237 @@
     )
 
 
-def sum_by_exchange(partial, axes, count):
-    rows = partial.shape[0] // count
-    pieces = lax.all_to_all(
-        partial.reshape((count, rows) + partial.shape[1:]), axes, split_axis=0, concat_axis=0
-    )
-    return gather_by_exchange(jnp.sum(pieces, axis=0), axes, count).reshape(partial.shape)
+def peer_copy(axis, count, step, source, target, sems):
+    peer = lax.rem(lax.axis_index(axis) + step, count)
+    return pltpu.make_async_remote_copy(
+        src_ref=source(peer),
+        dst_ref=target,
+        send_sem=sems[0].at[step],
+        recv_sem=sems[1].at[step],
+        device_id={axis: peer},
+        device_id_type=pl.DeviceIdType.MESH,
+    )
+
+
+def start_all(axis, count, source, target, sems):
+    def body(step, carry):
+        peer_copy(axis, count, step, source, target, sems).start()
+        return carry
+
+    lax.fori_loop(1, count, body, 0)
+
+
+def wait_all(axis, count, source, target, sems):
+    def body(step, carry):
+        peer_copy(axis, count, step, source, target, sems).wait()
+        return carry
+
+    lax.fori_loop(1, count, body, 0)
+
+
+def exchange(axis, count, source, target, sems):
+    start_all(axis, count, source, target, sems)
+    wait_all(axis, count, source, target, sems)
+
+
+def slot_sum(buffer, count):
+    if count <= 16:
+        total = buffer[0]
+        for slot in range(1, count):
+            total = total + buffer[slot]
+        return total
+    return lax.fori_loop(1, count, lambda slot, total: total + buffer[slot], buffer[0])
+
+
+def greet(box_size, col_size):
+    barrier = pltpu.get_barrier_semaphore()
+    for axis, count in (("box", box_size), ("col", col_size)):
+
+        def body(step, carry):
+            peer = lax.rem(lax.axis_index(axis) + step, count)
+            pl.semaphore_signal(
+                barrier, inc=1, device_id={axis: peer}, device_id_type=pl.DeviceIdType.MESH
+            )
+            return carry
+
+        lax.fori_loop(1, count, body, 0)
+    pl.semaphore_wait(barrier, box_size + col_size - 2)
+
+
+def nt_dot(left, right):
+    return lax.dot_general(
+        left,
+        right,
+        (((1,), (1,)), ((), ())),
+        precision=HIGHEST,
+        preferred_element_type=jnp.float32,
+    )
+
+
+def nn_dot(left, right):
+    return jnp.dot(left, right, precision=HIGHEST, preferred_element_type=jnp.float32)
+
+
+def factor_rows(matrix, size):
+    row_index = lax.broadcasted_iota(jnp.int32, matrix.shape, 0)
+    scale = jnp.zeros((size, 1), jnp.float32)
+    row_column = lax.broadcasted_iota(jnp.int32, (size, 1), 0)
+    for step in range(size):
+        pivot = matrix[step : step + 1, step : step + 1]
+        row = matrix[step : step + 1, :] * (1.0 / pivot)
+        column = matrix[:, step : step + 1]
+        scale = jnp.where(row_column == step, pivot, scale)
+        matrix = matrix - jnp.where(row_index > step, column * row, 0.0)
+    return matrix * lax.rsqrt(scale)
+
+
+def tail_kernel(
+    box_size,
+    col_size,
+    basis_ref,
+    applied_ref,
+    block_ref,
+    coupling_ref,
+    factor_ref,
+    row_basis,
+    row_applied,
+    part,
+    col_parts,
+    box_parts,
+    piece,
+    whole,
+    gram_mine,
+    gram_cols,
+    gram_sum,
+    gram_boxes,
+    normal,
+    *sems,
+):
+    sems = [(sems[2 * i], sems[2 * i + 1]) for i in range(8)]
+    prior, _, columns, _ = basis_ref.shape
+    all_columns, points = row_applied.shape[1:]
+    col = lax.axis_index("col")
+    box = lax.axis_index("box")
+    share = all_columns // col_size
+    row_total = points * box_size * col_size
+
+    def rows_of(index, size):
+        return pl.ds(pl.multiple_of(index * size, size), size)
+
+    def basis_source(peer):
+        return basis_ref.at[:, :, :, rows_of(peer, points)]
+
+    def applied_source(peer):
+        return applied_ref.at[:, :, rows_of(peer, points)]
+
+    basis_target = row_basis.at[:, :, rows_of(col, columns), :]
+    applied_target = row_applied.at[:, rows_of(col, columns), :]
+    greet(box_size, col_size)
+    start_all("col", col_size, applied_source, applied_target, sems[1])
+    start_all("col", col_size, basis_source, basis_target, sems[0])
+    row_basis[:, :, rows_of(col, columns), :] = basis_ref[:, :, :, rows_of(col, points)]
+    row_applied[:, rows_of(col, columns), :] = applied_ref[:, :, rows_of(col, points)]
+    wait_all("col", col_size, applied_source, applied_target, sems[1])
+    wait_all("col", col_size, basis_source, basis_target, sems[0])
+    flat_basis = jnp.concatenate(
+        [
+            row_basis[:, part_index].reshape(prior * all_columns, points)
+            for part_index in range(2)
+        ],
+        axis=1,
+    )
+    flat_applied = jnp.concatenate([row_applied[0], row_applied[1]], axis=1)
+    part[...] = nt_dot(flat_applied, flat_basis) * (1.0 / row_total)
+    col_parts[col] = part[rows_of(col, share), :]
+    exchange(
+        "col", col_size, lambda peer: part.at[rows_of(peer, share), :], col_parts.at[col], sems[2]
+    )
+    piece[...] = slot_sum(col_parts, col_size)
+    box_parts[box] = piece[...]
+    exchange("box", box_size, lambda peer: piece, box_parts.at[box], sems[3])
+    shared = slot_sum(box_parts, box_size)
+    whole[rows_of(col, share), :] = shared
+    piece[...] = shared
+    exchange("col", col_size, lambda peer: piece, whole.at[rows_of(col, share), :], sems[4])
+    coupling = whole[...]
+    residual = flat_applied - nn_dot(coupling, flat_basis)
+    blank = jnp.zeros_like(residual)
+    gram_mine[...] = nt_dot(residual, jnp.concatenate([residual, blank], axis=0)) * (
+        1.0 / row_total
+    )
+    gram_cols[col] = gram_mine[...]
+    gram_source = lambda peer: gram_mine
+    start_all("col", col_size, gram_source, gram_cols.at[col], sems[5])
+    coupling_ref[...] = coupling.T
+    wait_all("col", col_size, gram_source, gram_cols.at[col], sems[5])
+    gram_sum[...] = slot_sum(gram_cols, col_size)
+    gram_boxes[box] = gram_sum[...]
+    exchange("box", box_size, lambda peer: gram_sum, gram_boxes.at[box], sems[6])
+    gram = slot_sum(gram_boxes, box_size)
+    row_index = lax.broadcasted_iota(jnp.int32, gram.shape, 0)
+    lane_index = lax.broadcasted_iota(jnp.int32, gram.shape, 1)
+    trace = jnp.sum(jnp.where(row_index == lane_index, gram, 0.0), keepdims=True)
+    shift = trace * (SHIFT_SCALE / all_columns) + EPSILON
+    matrix = gram + jnp.where(row_index == lane_index, shift, 0.0)
+    matrix = matrix + jnp.where(row_index + all_columns == lane_index, 1.0, 0.0)
+    reduced = factor_rows(matrix, all_columns)
+    factor_ref[...] = jnp.where(lane_index >= row_index, reduced, 0.0)
+    inverse = jnp.where(lane_index >= all_columns, reduced, 0.0)
+    normalized = nn_dot(inverse, jnp.concatenate([blank, residual], axis=0))
+    normal[0] = normalized[:, :points]
+    normal[1] = normalized[:, points:]
+    block_ref[:, :, rows_of(col, points)] = normal[:, rows_of(col, columns), :]
+    exchange(
+        "col",
+        col_size,
+        lambda peer: normal.at[:, rows_of(peer, columns), :],
+        block_ref.at[:, :, rows_of(col, points)],
+        sems[7],
+    )
+
+
+def tail(basis, applied):
+    prior, parts, columns, local_points = basis.shape
+    box_size, col_size = lax.axis_size("box"), lax.axis_size("col")
+    all_columns, points = columns * col_size, local_points // col_size
+    share = all_columns // col_size
+    flat = prior * all_columns
+    square = (all_columns, 2 * all_columns)
+    shapes = [
+        (prior, parts, all_columns, points),
+        (parts, all_columns, points),
+        (all_columns, flat),
+        (col_size, share, flat),
+        (box_size, share, flat),
+        (share, flat),
+        (all_columns, flat),
+        square,
+        (col_size,) + square,
+        square,
+        (box_size,) + square,
+        (parts, all_columns, points),
+    ]
+    sems = []
+    for axis in ("col", "col", "col", "box", "col", "col", "box", "col"):
+        count = box_size if axis == "box" else col_size
+        sems += [pltpu.SemaphoreType.DMA((count,))] * 2
+    vmem = pl.BlockSpec(memory_space=pltpu.VMEM)
+    block, coupling, factor = pl.pallas_call(
+        functools.partial(tail_kernel, box_size, col_size),
+        out_shape=(
+            jax.ShapeDtypeStruct((parts, columns, local_points), jnp.float32),
+            jax.ShapeDtypeStruct((flat, all_columns), jnp.float32),
+            jax.ShapeDtypeStruct(square, jnp.float32),
+        ),
+        in_specs=[vmem] * 2,
+        out_specs=(vmem,) * 3,
+        scratch_shapes=[pltpu.VMEM(shape, jnp.float32) for shape in shapes] + sems,
+        compiler_params=pltpu.CompilerParams(
+            collective_id=0, has_side_effects=True, vmem_limit_bytes=40 * 1024 * 1024
+        ),
+    )(basis, applied)
+    coupling = coupling.reshape(prior, all_columns, all_columns)
+    return block, coupling, factor[:, :all_columns]
 
 
 def shards(basis, offsets, weights, interp, skeleton, near_boxes, near_count):
@@ -107,11 +335,9 @@
     columns = basis.shape[2]
     box_size = lax.axis_size("box")
     total_boxes = box_count * box_size
-    devices = box_size * lax.axis_size("col")
     first_box = lax.axis_index("box") * box_count
     own_boxes = first_box + jnp.arange(box_count, dtype=jnp.int32)
     positions = offsets.reshape(3, box_count, points) + box_centers(own_boxes)[:, :, None]
-    rows_basis = lax.all_to_all(basis, "col", split_axis=3, concat_axis=2, tiled=True)
     current = basis[prior_blocks - 1]
     sources = (current * weights).reshape(2, columns, box_count, points)
     payload = jnp.concatenate([sources.reshape(2 * columns, box_count, points), positions], axis=0)
@@ -155,30 +381,7 @@
     potentials = potentials.reshape(2, columns, box_count, skel_count)
     far_field = jnp.einsum("bkq,pcbk->pcbq", interp, potentials, precision=HIGHEST)
     applied = 0.5 * current + (near_field + far_field).reshape(2, columns, box_count * points)
-    rows_applied = lax.all_to_all(applied, "col", split_axis=2, concat_axis=1, tiled=True)
-    all_columns = rows_applied.shape[1]
-    row_total = rows_applied.shape[2] * devices
-    part_coupling = (
-        jnp.einsum("kpiq,pjq->kij", rows_basis, rows_applied, precision=HIGHEST) / row_total
-    ).reshape(prior_blocks * all_columns, all_columns)
-
-    def total(partial):
-        if partial.shape[0] % devices == 0 and devices <= 64:
-            return sum_by_exchange(partial, ("box", "col"), devices)
-        return lax.psum(partial, ("box", "col"))
-
-    coupling = total(part_coupling).reshape(prior_blocks, all_columns, all_columns)
-    residual = rows_applied - jnp.einsum("kpiq,kij->pjq", rows_basis, coupling, precision=HIGHEST)
-    gram_matrix = total(
-        jnp.einsum("piq,pjq->ij", residual, residual, precision=HIGHEST) / row_total
-    )
-    identity = jnp.eye(all_columns, dtype=jnp.float32)
-    shift_term = SHIFT_SCALE * jnp.trace(gram_matrix) / all_columns + EPSILON
-    lower_factor = jnp.linalg.cholesky(gram_matrix + shift_term * identity)
-    inverse = jax.scipy.linalg.solve_triangular(lower_factor, identity, lower=True)
-    normalized = jnp.einsum("ij,pjq->piq", inverse, residual, precision=HIGHEST)
-    new_block = lax.all_to_all(normalized, "col", split_axis=1, concat_axis=2, tiled=True)
-    return (new_block, coupling, lower_factor.T)
+    return tail(basis, applied)
 
 
 def solution(mesh):

time: 133 us -> 83.2 us (0.63)
  Pallas kernels: 0 us -> 38.2 us
  blocking collectives: 22.6 us -> 0 us
  other arithmetic: 33.5 us -> 14.9 us
  waiting for transfers between devices: 16.7 us -> 0.01 us
  starting transfers between devices: 28.5 us -> 13 us
  local copies, waits for them, and re-layouts: 20 us -> 7.58 us
  matrix products: 8.99 us -> 7.48 us
    pallas_call x0 -> x1, Pallas kernels: none -> 38.2 us  [tail(): pl.pallas_call(functools.partial(tail_kernel, box_size, col_size), out_sh...]
    all_to_all x2 -> x0, blocking collectives: 22.6 us -> none  [sum_by_exchange(): lax.all_to_all(partial.reshape((count, rows) + partial.shape[1:]), axes,...]
    all_to_all x3 -> x1, waiting for transfers between devices: 13.3 us -> 0.01 us  [gather_by_exchange(): lax.all_to_all(jnp.broadcast_to(piece[None], (count,) + piece.shape), axe...]
    another operation x4 -> x0, other arithmetic: 11.4 us -> none  [the longest x3 6.52 us: shards(): lower_factor = jnp.linalg.cholesky(gram_matrix + shift_term * identity)]
    all_to_all x3 -> x0, starting transfers between devices: 10.2 us -> none  [the longest x1 3.6 us: shards(): lax.all_to_all(basis, 'col', split_axis=3, concat_axis=2, tiled=True)]
    unnamed x27 -> x12, local copies, waits for them, and re-layouts: 11.3 us -> 3.4 us
    all_to_all x6 -> x0, other arithmetic: 5.41 us -> none  [the longest x2 1.57 us: sum_by_exchange(): lax.all_to_all(partial.reshape((count, rows) + partial.shape[1:]), axes,...]
    all_to_all x3 -> x1, starting transfers between devices: 10.9 us -> 6.22 us  [gather_by_exchange(): lax.all_to_all(jnp.broadcast_to(piece[None], (count,) + piece.shape), axe...]
  transfers between devices with their start and end apart: 8 -> 3, of which waited for: 3 -> 0; matrix products, arithmetic and copies ran while one was open for 28% -> 26% of each run, Pallas kernels for 0% -> 0%
where the time goes in v2:
time: 83.2 us; the launch traced here: 82.2 us
  Pallas kernels  38.2 us (46%)
  other arithmetic  14.9 us (18%)
  starting transfers between devices  13 us (16%)
  local copies, waits for them, and re-layouts  7.58 us (9%)
  matrix products  7.48 us (9%)
  between operations  0.99 us (1%)
    pallas_call x1, Pallas kernels, tail(): pl.pallas_call(functools.partial(tail_kernel, box_size, col_size), out_sh...  38.2 us
    mul x1, other arithmetic, helmholtz_pair(): jnp.cos(WAVENUMBER * distance) * factor  10.3 us
    all_to_all x1, starting transfers between devices, gather_by_exchange(): lax.all_to_all(jnp.broadcast_to(piece[None], (count,) + piece.shape), axe...  6.22 us
    ppermute x1, starting transfers between devices, extended_2(): lax.ppermute(tail, axis, [(i, (i + 1) % count) for i in range(ends)])  5.5 us
    dot_general x1, matrix products, shards(): jnp.einsum('gbtq,pcbq->gpcbt', stacked, source_val, precision=HIGHEST)  4.45 us
    unnamed x12, local copies, waits for them, and re-layouts  3.4 us
    mul x1, other arithmetic, far_block(): kernel_re.reshape(target_count, source_boxes, skel_count)  2.34 us
  transfers between devices with their start and end apart: 3, of which 0 were waited for; matrix products, arithmetic and copies ran while one was open for 26% of the time, Pallas kernels for 0%

profile of v2, /device:TPU:0, one launch (start us, length us, event | category | flops | bytes accessed | tf_op | source)
XLA Modules:
  0.0 82.2 jit_solution(15918301311997838612)
XLA Ops:
  0.7 0.7 reshape.722
  1.4 0.8 %slice.103 = f32[1,2,16,512]{3,2,1,0:T(8,128)S(1)} slice(f32[4,2,16,512]{3,2,1,0:T(8,128)} %basis_ref.1), slice={[3:4], [0:2], [0:16], [0:512]} | slice | bytes 131072 | tf_op jit(solution)/shard_map/slice | solution.py:341
  2.5 0.7 broadcast.561
  3.2 1.3 %collective-permute-start.1 = (f32[35,4,128]{2,1,0:T(4,128)S(1)}, f32[35,4,128]{2,1,0:T(4,128)S(1)}, u32[]{:S(2)}, u32[]{:S(2)}) collective-permute-start(f32[35,4,128]{2,1,0:T(4,128)S(1)} %pad_maximum_fusion.2), channel_id=1, source_target_pairs={{4,0},{8,4},{12,8},{16,12},{20,16},{24,20},{28,24},{5,1},{9,5},{13... | collective-permute-start | bytes 215048 | tf_op jit(solution)/shard_map/ppermute | solution.py:32
  4.5 5.5 %collective-permute-start = (f32[35,4,128]{2,1,0:T(4,128)S(1)}, f32[35,4,128]{2,1,0:T(4,128)S(1)}, u32[]{:S(2)}, u32[]{:S(2)}) collective-permute-start(f32[35,4,128]{2,1,0:T(4,128)S(1)} %pad_maximum_fusion.2), channel_id=1, source_target_pairs={{0,4},{4,8},{8,12},{12,16},{16,20},{20,24},{24,28},{1,5},{5,9},{9,... | collective-permute-start | bytes 215048 | tf_op jit(solution)/shard_map/ppermute | solution.py:30
  10.0 0.9 %convolution_bitcast_fusion.3 = f32[3,4,32]{2,0,1:T(4,128)S(1)} fusion(s32[4,32]{1,0:T(4,128)} %param.11, f32[3,4,128]{2,1,0:T(4,128)S(1)} %broadcast_add_fusion.1), kind=kOutput, calls=%fused_computation.15 | convolution fusion | flops 606208 | bytes 8192 | tf_op jit(solution)/shard_map/bkq,dbq->dbk/dot_general | solution.py:349
  11.0 0.9 %convolution_bitcast_fusion.1 = f32[2,16,4,32]{3,1,0,2:T(8,128)S(1)} fusion(f32[4,32,128]{2,1,0:T(8,128)S(1)} %copy-done, f32[2,16,4,128]{3,2,1,0:T(4,128)S(1)} %squeeze.5, f32[4,128]{1,0:T(4,128)} %bitcast.136), kind=kOutput, calls=%fused_computation.13 | convolution fusion | flops 6307840 | bytes 149504 | tf_op jit(solution)/shard_map/bkq,pcbq->pcbk/dot_general | solution.py:345
  12.1 0.7 broadcast_in_dim.4
  12.8 6.2 %all-to-all-start = ((f32[8,35,128]{2,1,0:T(8,128)}), f32[8,35,128]{2,1,0:T(8,128)S(1)}, u32[]{:S(2)}, u32[]{:S(2)}) async-start(f32[8,35,128]{2,1,0:T(8,128)} %broadcast_in_dim.4), calls=%async_computation | async-start | bytes 327680 | tf_op jit(solution)/shard_map/all_to_all | solution.py:91
  19.0 0.7 iota_compare_fusion.3
  19.8 0.8 copy.64
  20.6 0.8 %convert_reduce_fusion = f32[4,9]{0,1:T(8,128)S(1)} fusion(s32[4,9]{0,1:T(8,128)S(1)} %broadcast_add_fusion, s32[4,27]{1,0:T(4,128)} %param.12, pred[4,27]{1,0:T(4,128)(4,1)S(1)} %copy.54), kind=kLoop, calls=%fused_computation.59 | loop fusion | flops 3852 | bytes 828 | tf_op jit(solution)/shard_map/reduce_sum | solution.py:362
  22.3 0.2 copy.66
  22.8 0.2 slice_multiply_fusion
  23.0 0.2 reshape.733
  23.3 10.3 %cosine_multiply_fusion = (f32[1,4,128,1152]{3,2,0,1:T(8,128)S(1)}, f32[1,4,128,1152]{3,2,0,1:T(8,128)S(1)}) fusion(f32[4,1152]{1,0:T(4,128)S(1)} %bitcast.129, f32[4,128]{1,0:T(4,128)S(1)} %get-tuple-element.29, f32[4,1152]{1,0:T(4,128)S(1)} %bitcast.130, f32[4,128]{1,0:T(4,128)S(1)} %get-tuple-element.30, f32[4,1152]{1,0:T(4,128)S(1)} %bitcast.128, ...), kind=kLoop, calls=%fused_computation.6 | loop fusion | flops 8257536 | bytes 4780032 | tf_op jit(solution)/shard_map/mul | solution.py:53
  33.6 4.4 %fusion.3 = f32[2,2,16,4,128]{4,2,0,1,3:T(8,128)S(1)} fusion(f32[1,4,128,1152]{3,2,0,1:T(8,128)S(1)} %get-tuple-element.25, f32[1,4,128,1152]{3,2,0,1:T(8,128)S(1)} %get-tuple-element.24, f32[2,16,4,1152,1]{3,2,1,0,4:T(4,128)S(1)} %bitcast.121), kind=kOutput, calls=%fused_computation.9 | convolution fusion | flops 454164480 | bytes 5439488 | tf_op jit(solution)/shard_map/gbtq,pcbq->gpcbt/dot_general | solution.py:370
  38.3 2.3 %multiply_multiply_fusion.1 = (f32[1,128,1024]{2,1,0:T(8,128)S(1)}, f32[1,128,1024]{2,1,0:T(8,128)S(1)}) fusion(f32[1,128,1024]{2,1,0:T(8,128)S(1)} %copy.66, f32[1024]{0:T(1024)S(1)} %bitcast.132, f32[128]{0:T(128)S(1)} %sub.245, f32[1024]{0:T(1024)S(1)} %bitcast.133, f32[128]{0:T(128)S(1)} %sub.240, f32[1024]{0:T(1024)S(1)} %bitcast.131, f32[128]{0:T(128)S(1)} %sub.235), kind=kLoop, calls=%fused_computation.22 | loop fusion | flops 2097152 | bytes 1586688 | tf_op jit(solution)/shard_map/mul | solution.py:64
  40.6 1.0 %convolution_bitcast_fusion.2 = f32[2,2,16,128]{3,2,0,1:T(8,128)S(1)} fusion(f32[1,128,1024]{2,1,0:T(8,128)S(1)} %get-tuple-element.16, f32[1,128,1024]{2,1,0:T(8,128)S(1)} %get-tuple-element.15, f32[2,16,1024,1]{2,1,0,3:T(8,128)S(1)} %reshape.731), kind=kOutput, calls=%fused_computation.14 | convolution fusion | flops 100925440 | bytes 1212416 | tf_op jit(solution)/shard_map/gts,pcs->gpct/dot_general | solution.py:71
  41.9 0.2 fusion.5
  42.1 38.2 %shard_map.94 = (f32[2,16,512]{2,1,0:T(8,128)S(1)}, f32[256,64]{1,0:T(8,128)S(1)}, f32[64,128]{1,0:T(8,128)S(1)}) custom-call(f32[4,2,16,512]{3,2,1,0:T(8,128)S(1)} %copy-done.1, f32[2,16,512]{2,1,0:T(8,128)S(1)} %bitcast_add_fusion.applied_ref), custom_call_target="tpu_custom_call" | custom-call | tf_op jit(solution)/shard_map/pallas_call | solution.py:311
  80.3 0.6 copy.100
  81.0 0.7 copy.101
  81.6 0.6 copy.102
  (55 shorter events, 2.2 us)
Async XLA Ops:
  0.6 10.4 %copy-start = (f32[4,32,128]{2,1,0:T(8,128)S(1)}, f32[4,32,128]{2,1,0:T(8,128)}, u32[]{:S(2)}) copy-start(f32[4,32,128]{2,1,0:T(8,128)} %param.10) | copy-start | bytes 196612
  3.2 19.3 %collective-permute-start.1 = (f32[35,4,128]{2,1,0:T(4,128)S(1)}, f32[35,4,128]{2,1,0:T(4,128)S(1)}, u32[]{:S(2)}, u32[]{:S(2)}) collective-permute-start(f32[35,4,128]{2,1,0:T(4,128)S(1)} %pad_maximum_fusion.2), channel_id=1, source_target_pairs={{4,0},{8,4},{12,8},{16,12},{20,16},{24,20},{28,24},{5,1},{9,5},{13... | collective-permute-start | bytes 215048 | tf_op jit(solution)/shard_map/ppermute | solution.py:32
  4.5 18.1 %collective-permute-start = (f32[35,4,128]{2,1,0:T(4,128)S(1)}, f32[35,4,128]{2,1,0:T(4,128)S(1)}, u32[]{:S(2)}, u32[]{:S(2)}) collective-permute-start(f32[35,4,128]{2,1,0:T(4,128)S(1)} %pad_maximum_fusion.2), channel_id=1, source_target_pairs={{0,4},{4,8},{8,12},{12,16},{16,20},{20,24},{24,28},{1,5},{5,9},{9,... | collective-permute-start | bytes 215048 | tf_op jit(solution)/shard_map/ppermute | solution.py:30
  12.8 25.3 %all-to-all-start = ((f32[8,35,128]{2,1,0:T(8,128)}), f32[8,35,128]{2,1,0:T(8,128)S(1)}, u32[]{:S(2)}, u32[]{:S(2)}) async-start(f32[8,35,128]{2,1,0:T(8,128)} %broadcast_in_dim.4), calls=%async_computation | async-start | bytes 327680 | tf_op jit(solution)/shard_map/all_to_all | solution.py:91
  38.1 4.0 %copy-start.1 = (f32[4,2,16,512]{3,2,1,0:T(8,128)S(1)}, f32[4,2,16,512]{3,2,1,0:T(8,128)}, u32[]{:S(2)}) copy-start(f32[4,2,16,512]{3,2,1,0:T(8,128)} %basis_ref.1) | copy-start | bytes 786436

commit v3 on v2

v3 whole, which is shorter than its diff:
```python
import functools
import math

import jax
import jax.numpy as jnp
from jax import lax
from jax.experimental import pallas as pl
from jax.experimental.pallas import tpu as pltpu
from jax.sharding import PartitionSpec as P

BOX_DEV = 4


WAVENUMBER = 6.0
SMOOTHING = 0.1
SHIFT_SCALE = 0.02
EPSILON = 1e-06
HIGHEST = lax.Precision.HIGHEST


def split(values):
    high = values.astype(jnp.bfloat16)
    return high, (values - high.astype(jnp.float32)).astype(jnp.bfloat16)


def pair_dot(values, kernel):
    rows = values.shape[0]
    value_high, value_low = split(values)
    kernel_high, kernel_low = split(kernel)
    both = jnp.dot(
        jnp.concatenate([value_high, value_low], axis=0),
        kernel_high,
        preferred_element_type=jnp.float32,
    )
    cross = jnp.dot(value_high, kernel_low, preferred_element_type=jnp.float32)
    return both[:rows] + both[rows:] + cross


def helmholtz_pair(sources, targets):
    spread = SMOOTHING * SMOOTHING
    for axis_index in range(3):
        step = sources[:, axis_index : axis_index + 1] - targets[axis_index : axis_index + 1, :]
        spread = spread + step * step
    inverse = lax.rsqrt(spread)
    angle = WAVENUMBER * (spread * inverse)
    factor = inverse * (1.0 / (4.0 * math.pi))
    turns = jnp.floor(angle * (2.0 / math.pi) + 0.5)
    quarter = turns.astype(jnp.int32)
    rest = angle - turns * 1.5703125
    rest = rest - turns * 4.837512969970703125e-4
    rest = rest - turns * 7.54978995489188216e-8
    square = rest * rest
    sine = (-1.9515295891e-4 * square + 8.3321608736e-3) * square - 1.6666654611e-1
    sine = sine * square * rest + rest
    cosine = (2.443315711809948e-5 * square - 1.388731625493765e-3) * square
    cosine = (cosine + 4.166664568298827e-2) * square * square - 0.5 * square + 1.0
    odd = (quarter & 1) == 1
    sine, cosine = jnp.where(odd, cosine, sine), jnp.where(odd, sine, cosine)
    sine_factor = jnp.where((quarter & 2) == 2, -factor, factor)
    cosine_factor = jnp.where(((quarter + 1) & 2) == 2, -factor, factor)
    return cosine * cosine_factor, sine * sine_factor


def combine(product, columns, points):
    left, right = product[:, :points], product[:, points:]
    return jnp.concatenate(
        [left[:columns] - right[columns:], left[columns:] + right[:columns]], axis=0
    )


def peer_copy(axis, count, step, source, target, sems):
    peer = lax.rem(lax.axis_index(axis) + step, count)
    return pltpu.make_async_remote_copy(
        src_ref=source(peer),
        dst_ref=target,
        send_sem=sems[0].at[step],
        recv_sem=sems[1].at[step],
        device_id={axis: peer},
        device_id_type=pl.DeviceIdType.MESH,
    )


def start_all(axis, count, source, target, sems):
    def body(step, carry):
        peer_copy(axis, count, step, source, target, sems).start()
        return carry

    lax.fori_loop(1, count, body, 0)


def wait_all(axis, count, source, target, sems):
    def body(step, carry):
        peer_copy(axis, count, step, source, target, sems).wait()
        return carry

    lax.fori_loop(1, count, body, 0)


def exchange(axis, count, source, target, sems):
    start_all(axis, count, source, target, sems)
    wait_all(axis, count, source, target, sems)


def slot_sum(buffer, count):
    if count <= 16:
        total = buffer[0]
        for slot in range(1, count):
            total = total + buffer[slot]
        return total
    return lax.fori_loop(1, count, lambda slot, total: total + buffer[slot], buffer[0])


def greet(barrier, box_size, col_size):
    for axis, count in (("box", box_size), ("col", col_size)):

        def body(step, carry):
            peer = lax.rem(lax.axis_index(axis) + step, count)
            pl.semaphore_signal(
                barrier, inc=1, device_id={axis: peer}, device_id_type=pl.DeviceIdType.MESH
            )
            return carry

        lax.fori_loop(1, count, body, 0)


def nt_dot(left, right):
    return lax.dot_general(
        left,
        right,
        (((1,), (1,)), ((), ())),
        precision=HIGHEST,
        preferred_element_type=jnp.float32,
    )


def nn_dot(left, right):
    return jnp.dot(left, right, precision=HIGHEST, preferred_element_type=jnp.float32)


def factor_rows(matrix, size):
    row_index = lax.broadcasted_iota(jnp.int32, matrix.shape, 0)
    scale = jnp.zeros((size, 1), jnp.float32)
    row_column = lax.broadcasted_iota(jnp.int32, (size, 1), 0)
    for step in range(size):
        pivot = matrix[step : step + 1, step : step + 1]
        row = matrix[step : step + 1, :] * (1.0 / pivot)
        column = matrix[:, step : step + 1]
        scale = jnp.where(row_column == step, pivot, scale)
        matrix = matrix - jnp.where(row_index > step, column * row, 0.0)
    return matrix * lax.rsqrt(scale)


def step_kernel(
    box_size,
    col_size,
    basis_ref,
    offsets_ref,
    weights_ref,
    interp_ref,
    skeleton_ref,
    near_boxes_ref,
    near_count_ref,
    block_ref,
    coupling_ref,
    factor_ref,
    row_basis,
    row_applied,
    part,
    col_parts,
    box_parts,
    piece,
    whole,
    gram_mine,
    gram_cols,
    gram_sum,
    gram_boxes,
    normal,
    applied_ref,
    beside,
    column_pos,
    far_mine,
    far_all,
    near_times,
    far_times,
    near_total,
    far_total,
    *sems,
):
    sems = [(sems[2 * i], sems[2 * i + 1]) for i in range(11)]
    prior, _, columns, _ = basis_ref.shape
    all_columns, points = row_applied.shape[1:]
    col = lax.axis_index("col")
    box = lax.axis_index("box")
    share = all_columns // col_size
    row_total = points * box_size * col_size

    def rows_of(index, size):
        return pl.ds(pl.multiple_of(index * size, size), size)

    def basis_source(peer):
        return basis_ref.at[:, :, :, rows_of(peer, points)]

    def applied_source(peer):
        return applied_ref.at[:, :, rows_of(peer, points)]

    basis_target = row_basis.at[:, :, rows_of(col, columns), :]
    applied_target = row_applied.at[:, rows_of(col, columns), :]
    box_count, skel_count, box_points = interp_ref.shape
    rows = 2 * columns
    reach = box_count
    window = 2 * reach + 1
    first_box = box * box_count
    barrier = pltpu.get_barrier_semaphore()
    greet(barrier, box_size, col_size)

    def of_box(index):
        return slice(index * box_points, (index + 1) * box_points)

    local_points = box_count * box_points
    box_lane = lax.broadcasted_iota(jnp.int32, (1, local_points), 1) // box_points + first_box
    center_first = (box_lane // BOX_DEV).astype(jnp.float32)
    center_second = (box_lane % BOX_DEV).astype(jnp.float32)
    positions = jnp.concatenate(
        [
            offsets_ref[0:1, :] + center_first,
            offsets_ref[1:2, :] + center_second,
            offsets_ref[2:3, :],
            jnp.zeros((5, local_points), jnp.float32),
        ],
        axis=0,
    )
    current = basis_ref[prior - 1].reshape(rows, local_points)
    sources = current * weights_ref[...]
    beside[1, :rows, :] = sources
    beside[1, rows:, :] = positions
    pl.semaphore_wait(barrier, box_size + col_size - 2)
    after = lax.rem(box + 1, box_size)
    before = lax.rem(box + box_size - 1, box_size)
    side_copies = [
        pltpu.make_async_remote_copy(
            src_ref=beside.at[1],
            dst_ref=beside.at[slot],
            send_sem=sems[index][0].at[0],
            recv_sem=sems[index][1].at[0],
            device_id={"box": peer},
            device_id_type=pl.DeviceIdType.MESH,
        )
        for slot, peer, index in ((0, after, 8), (2, before, 9))
    ]
    for copy in side_copies:
        copy.start()
    flat_skel = box_count * skel_count
    interp = interp_ref[...].reshape(flat_skel, box_points)
    skel_box = lax.broadcasted_iota(jnp.int32, (1, flat_skel), 1) // skel_count
    skel_flat = jnp.concatenate([skeleton_ref[b : b + 1, :] for b in range(box_count)], axis=1)
    hot = (
        lax.broadcasted_iota(jnp.int32, (box_points, flat_skel), 0) == skel_flat
    ).astype(jnp.float32)
    charges = jnp.zeros((rows, flat_skel), jnp.float32)
    skel_pos = jnp.zeros((8, flat_skel), jnp.float32)
    stacked = nt_dot(
        jnp.concatenate([sources[:, of_box(b)] for b in range(box_count)], axis=0), interp
    )
    stacked_pos = nn_dot(
        jnp.concatenate([positions[:, of_box(b)] for b in range(box_count)], axis=0), hot
    )
    for b in range(box_count):
        charges = jnp.where(skel_box == b, stacked[b * rows : (b + 1) * rows], charges)
        skel_pos = jnp.where(skel_box == b, stacked_pos[b * 8 : (b + 1) * 8], skel_pos)
    far_mine[:rows, :] = charges
    far_mine[rows:, :] = skel_pos
    far_all[box] = far_mine[...]
    far_source = lambda peer: far_mine
    start_all("box", box_size, far_source, far_all.at[box], sems[10])
    start_all("col", col_size, basis_source, basis_target, sems[0])
    own_box = lax.broadcasted_iota(jnp.int32, (box_count, 1), 0) + first_box
    slots = lax.broadcasted_iota(jnp.int32, near_boxes_ref.shape, 1)
    distance = jnp.where(slots < near_count_ref[...], near_boxes_ref[...] - own_box, window)
    for o in range(window):
        times = jnp.sum((distance == o - reach).astype(jnp.float32), axis=1, keepdims=True)
        near_times[o] = jnp.broadcast_to(times, (box_count, box_points))
        listed = jnp.zeros((1, flat_skel), jnp.float32)
        for b in range(box_count):
            listed = jnp.where(skel_box == b, jnp.minimum(times[b : b + 1], 1.0), listed)
        far_times[o : o + 1, :] = listed
    near_total[...] = jnp.zeros_like(near_total)
    far_total[...] = jnp.zeros_like(far_total)
    for copy in side_copies:
        copy.wait()
    for slot in range(3):
        column_pos[slot * local_points : (slot + 1) * local_points, :] = beside[slot, rows:, :].T

    def near_step(o, carry):
        for b in range(box_count):
            extended = o + b
            lanes = rows_of(lax.rem(extended, box_count), box_points)
            values = beside[extended // box_count, :rows, lanes]
            values = values * near_times[o, b : b + 1, :]
            source_pos = column_pos[rows_of(extended, box_points), :]
            kernel = helmholtz_pair(source_pos, beside[1, rows:, of_box(b)])
            near_total[b] += pair_dot(values, jnp.concatenate(kernel, axis=1))
        return carry

    lax.fori_loop(0, window, near_step, 0)
    wait_all("box", box_size, far_source, far_all.at[box], sems[10])

    def far_step(slot, carry):
        source_pos = far_all[slot, rows:, :].T
        kernel_re, kernel_im = helmholtz_pair(source_pos, far_mine[rows:, :])
        source_box = lax.broadcasted_iota(jnp.int32, kernel_re.shape, 0) // skel_count
        offset = source_box + (slot * box_count - first_box + reach) - skel_box
        weight = jnp.ones_like(kernel_re)
        for o in range(window):
            weight = jnp.where(offset == o, 1.0 - far_times[o : o + 1, :], weight)
        kernel = jnp.concatenate([kernel_re * weight, kernel_im * weight], axis=1)
        far_total[...] += pair_dot(far_all[slot, :rows, :], kernel)
        return carry

    lax.fori_loop(0, box_size, far_step, 0)
    potentials = combine(far_total[...], columns, flat_skel)
    far_field = nn_dot(
        jnp.concatenate(
            [jnp.where(skel_box == b, potentials, 0.0) for b in range(box_count)], axis=0
        ),
        interp,
    )
    for b in range(box_count):
        field = combine(near_total[b], columns, box_points) + far_field[b * rows : (b + 1) * rows]
        field = 0.5 * current[:, of_box(b)] + field
        applied_ref[0, :, of_box(b)] = field[:columns]
        applied_ref[1, :, of_box(b)] = field[columns:]
    start_all("col", col_size, applied_source, applied_target, sems[1])
    row_basis[:, :, rows_of(col, columns), :] = basis_ref[:, :, :, rows_of(col, points)]
    row_applied[:, rows_of(col, columns), :] = applied_ref[:, :, rows_of(col, points)]
    wait_all("col", col_size, applied_source, applied_target, sems[1])
    wait_all("col", col_size, basis_source, basis_target, sems[0])
    flat_basis = jnp.concatenate(
        [
            row_basis[:, part_index].reshape(prior * all_columns, points)
            for part_index in range(2)
        ],
        axis=1,
    )
    flat_applied = jnp.concatenate([row_applied[0], row_applied[1]], axis=1)
    part[...] = nt_dot(flat_applied, flat_basis) * (1.0 / row_total)
    col_parts[col] = part[rows_of(col, share), :]
    exchange(
        "col", col_size, lambda peer: part.at[rows_of(peer, share), :], col_parts.at[col], sems[2]
    )
    piece[...] = slot_sum(col_parts, col_size)
    box_parts[box] = piece[...]
    exchange("box", box_size, lambda peer: piece, box_parts.at[box], sems[3])
    shared = slot_sum(box_parts, box_size)
    whole[rows_of(col, share), :] = shared
    piece[...] = shared
    exchange("col", col_size, lambda peer: piece, whole.at[rows_of(col, share), :], sems[4])
    coupling = whole[...]
    residual = flat_applied - nn_dot(coupling, flat_basis)
    blank = jnp.zeros_like(residual)
    gram_mine[...] = nt_dot(residual, jnp.concatenate([residual, blank], axis=0)) * (
        1.0 / row_total
    )
    gram_cols[col] = gram_mine[...]
    gram_source = lambda peer: gram_mine
    start_all("col", col_size, gram_source, gram_cols.at[col], sems[5])
    coupling_ref[...] = coupling.T
    wait_all("col", col_size, gram_source, gram_cols.at[col], sems[5])
    gram_sum[...] = slot_sum(gram_cols, col_size)
    gram_boxes[box] = gram_sum[...]
    exchange("box", box_size, lambda peer: gram_sum, gram_boxes.at[box], sems[6])
    gram = slot_sum(gram_boxes, box_size)
    row_index = lax.broadcasted_iota(jnp.int32, gram.shape, 0)
    lane_index = lax.broadcasted_iota(jnp.int32, gram.shape, 1)
    trace = jnp.sum(jnp.where(row_index == lane_index, gram, 0.0), keepdims=True)
    shift = trace * (SHIFT_SCALE / all_columns) + EPSILON
    matrix = gram + jnp.where(row_index == lane_index, shift, 0.0)
    matrix = matrix + jnp.where(row_index + all_columns == lane_index, 1.0, 0.0)
    reduced = factor_rows(matrix, all_columns)
    factor_ref[...] = jnp.where(lane_index >= row_index, reduced, 0.0)
    inverse = jnp.where(lane_index >= all_columns, reduced, 0.0)
    normalized = nn_dot(inverse, jnp.concatenate([blank, residual], axis=0))
    normal[0] = normalized[:, :points]
    normal[1] = normalized[:, points:]
    block_ref[:, :, rows_of(col, points)] = normal[:, rows_of(col, columns), :]
    exchange(
        "col",
        col_size,
        lambda peer: normal.at[:, rows_of(peer, columns), :],
        block_ref.at[:, :, rows_of(col, points)],
        sems[7],
    )


def shards(basis, offsets, weights, interp, skeleton, near_boxes, near_count):
    prior, parts, columns, local_points = basis.shape
    box_count, skel_count, box_points = interp.shape
    flat_skel = box_count * skel_count
    rows = parts * columns
    window = 2 * box_count + 1
    box_size, col_size = lax.axis_size("box"), lax.axis_size("col")
    all_columns, points = columns * col_size, local_points // col_size
    share = all_columns // col_size
    flat = prior * all_columns
    square = (all_columns, 2 * all_columns)
    shapes = [
        (prior, parts, all_columns, points),
        (parts, all_columns, points),
        (all_columns, flat),
        (col_size, share, flat),
        (box_size, share, flat),
        (share, flat),
        (all_columns, flat),
        square,
        (col_size,) + square,
        square,
        (box_size,) + square,
        (parts, all_columns, points),
        (parts, columns, local_points),
        (3, rows + 8, local_points),
        (3 * local_points, 8),
        (rows + 8, flat_skel),
        (box_size, rows + 8, flat_skel),
        (window, box_count, box_points),
        (window, flat_skel),
        (box_count, rows, 2 * box_points),
        (rows, 2 * flat_skel),
    ]
    sems = []
    for axis in ("col", "col", "col", "box", "col", "col", "box", "col", "", "", "box"):
        count = {"box": box_size, "col": col_size, "": 1}[axis]
        sems += [pltpu.SemaphoreType.DMA((count,))] * 2
    vmem = pl.BlockSpec(memory_space=pltpu.VMEM)
    block, coupling, factor = pl.pallas_call(
        functools.partial(step_kernel, box_size, col_size),
        out_shape=(
            jax.ShapeDtypeStruct((parts, columns, local_points), jnp.float32),
            jax.ShapeDtypeStruct((flat, all_columns), jnp.float32),
            jax.ShapeDtypeStruct(square, jnp.float32),
        ),
        in_specs=[vmem] * 7,
        out_specs=(vmem,) * 3,
        scratch_shapes=[pltpu.VMEM(shape, jnp.float32) for shape in shapes] + sems,
        compiler_params=pltpu.CompilerParams(
            collective_id=0, has_side_effects=True, vmem_limit_bytes=40 * 1024 * 1024
        ),
    )(
        basis,
        offsets,
        weights.reshape(1, local_points),
        interp,
        skeleton,
        near_boxes,
        near_count.reshape(box_count, 1),
    )
    coupling = coupling.reshape(prior, all_columns, all_columns)
    return block, coupling, factor[:, :all_columns]


def solution(mesh):
    return jax.shard_map(
        shards,
        mesh=mesh,
        in_specs=(
            P(None, None, "col", "box"),
            P(None, "box"),
            P("box"),
            P("box", None, None),
            P("box", None),
            P("box", None),
            P("box"),
        ),
        out_specs=(P(None, "col", "box"), P(), P()),
        check_vma=False,
    )
```

time: 83.2 us -> 62.6 us (0.75)
  Pallas kernels: 38.2 us -> 55.7 us
  other arithmetic: 14.9 us -> 0 us
  starting transfers between devices: 13 us -> 0 us
  matrix products: 7.48 us -> 0 us
  local copies, waits for them, and re-layouts: 7.58 us -> 5.15 us
    pallas_call x1, Pallas kernels: 38.2 us -> 55.7 us  [shards(): pl.pallas_call(functools.partial(step_kernel, box_size, col_size), out_sh...]
    mul x4 -> x0, other arithmetic: 12.8 us -> none  [the longest x1 10.3 us: helmholtz_pair(): jnp.cos(WAVENUMBER * distance) * factor]
    dot_general x5 -> x0, matrix products: 7.48 us -> none  [the longest x1 4.45 us: shards(): jnp.einsum('gbtq,pcbq->gpcbt', stacked, source_val, precision=HIGHEST)]
    ppermute x2 -> x0, starting transfers between devices: 6.8 us -> none  [the longest x1 5.5 us: extended_2(): lax.ppermute(tail, axis, [(i, (i + 1) % count) for i in range(ends)])]
    all_to_all x1 -> x0, starting transfers between devices: 6.22 us -> none  [gather_by_exchange(): lax.all_to_all(jnp.broadcast_to(piece[None], (count,) + piece.shape), axe...]
    unnamed x12 -> x15, local copies, waits for them, and re-layouts: 3.4 us -> 4.39 us
    slice x5 -> x0, local copies, waits for them, and re-layouts: 0.98 us -> none  [the longest x1 0.84 us: shards(): current = basis[prior_blocks - 1]]
    reduce_sum x1 -> x0, other arithmetic: 0.84 us -> none  [shards(): jnp.sum((listed & slot_live[:, :, None]).astype(jnp.float32), axis=1)]
  transfers between devices with their start and end apart: 3 -> 0, of which waited for: 0 -> 0; matrix products, arithmetic and copies ran while one was open for 26% -> 0% of each run, Pallas kernels for 0% -> 0%
where the time goes in v3:
time: 62.6 us; the launch traced here: 61.5 us
  Pallas kernels  55.7 us (89%)
  local copies, waits for them, and re-layouts  5.15 us (8%)
  between operations  0.68 us (1%)
    pallas_call x1, Pallas kernels, shards(): pl.pallas_call(functools.partial(step_kernel, box_size, col_size), out_sh...  55.7 us
    unnamed x15, local copies, waits for them, and re-layouts  4.39 us

profile of v3, /device:TPU:0, one launch (start us, length us, event | category | flops | bytes accessed | tf_op | source)
XLA Modules:
  0.0 61.5 jit_solution(3283507078827202377)
XLA Ops:
  0.6 0.0 copy-start.5
  0.6 0.0 copy-start.3
  0.7 0.0 copy-start.4
  0.7 0.8 %copy.10.near_count_ref = s32[4,1]{1,0:T(4,128)S(1)} copy(s32[4,1]{0,1:T(1,128)} %bitcast.7) | data formatting | bytes 32 | tf_op jit(solution)/shard_map/reshape | solution.py:453
  1.4 0.0 copy-done.5
  1.4 0.0 copy-done.3
  1.4 0.0 copy-done.4
  1.4 0.0 copy-start
  1.4 0.9 %copy-done = f32[4,2,16,512]{3,2,1,0:T(8,128)S(1)} copy-done((f32[4,2,16,512]{3,2,1,0:T(8,128)S(1)}, f32[4,2,16,512]{3,2,1,0:T(8,128)}, u32[]{:S(2)}) %copy-start) | copy-done | bytes 262168
  2.4 0.0 copy-start.1
  2.4 0.8 %copy-done.1 = f32[4,32,128]{2,1,0:T(8,128)S(1)} copy-done((f32[4,32,128]{2,1,0:T(8,128)S(1)}, f32[4,32,128]{2,1,0:T(8,128)}, u32[]{:S(2)}) %copy-start.1) | copy-done | bytes 65560
  3.2 0.0 copy-start.2
  3.2 0.7 %copy-done.2 = f32[3,512]{1,0:T(4,128)S(1)} copy-done((f32[3,512]{1,0:T(4,128)S(1)}, f32[3,512]{1,0:T(4,128)}, u32[]{:S(2)}) %copy-start.2) | copy-done | bytes 6168
  3.9 55.7 %shard_map.94 = (f32[2,16,512]{2,1,0:T(8,128)S(1)}, f32[256,64]{1,0:T(8,128)S(1)}, f32[64,128]{1,0:T(8,128)S(1)}) custom-call(f32[4,2,16,512]{3,2,1,0:T(8,128)S(1)} %copy-done, f32[3,512]{1,0:T(4,128)S(1)} %copy-done.2, f32[1,512]{1,0:T(1,128)S(1)} %bitcast.6, f32[4,32,128]{2,1,0:T(8,128)S(1)} %copy-done.1, s32[4,32]{1,0:T(4,128)S(1)} %copy-done.4, ...), custom_call_target="tpu_custom_call" | custom-call | tf_op jit(solution)/shard_map/pallas_call | solution.py:433
  59.6 0.6 %copy.14 = f32[2,16,512]{2,1,0:T(8,128)} copy(f32[2,16,512]{2,1,0:T(8,128)S(1)} %get-tuple-element.12) | data formatting | bytes 131072
  60.3 0.7 %copy.15 = f32[4,64,64]{2,1,0:T(8,128)} copy(f32[4,64,64]{2,1,0:T(8,128)S(1)} %bitcast.4) | data formatting | bytes 131072
  60.9 0.6 copy.16
Async XLA Ops:
  0.6 0.8 %copy-start.5 = (s32[4,27]{1,0:T(4,128)S(1)}, s32[4,27]{1,0:T(4,128)}, u32[]{:S(2)}) copy-start(s32[4,27]{1,0:T(4,128)} %near_boxes_ref.1) | copy-start | bytes 1300
  0.6 0.8 %copy-start.3 = (f32[512]{0:T(512)S(1)}, f32[512]{0:T(512)}, u32[]{:S(2)}) copy-start(f32[512]{0:T(512)} %param.9) | copy-start | bytes 6148
  0.7 0.8 %copy-start.4 = (s32[4,32]{1,0:T(4,128)S(1)}, s32[4,32]{1,0:T(4,128)}, u32[]{:S(2)}) copy-start(s32[4,32]{1,0:T(4,128)} %skeleton_ref.1) | copy-start | bytes 1540
  1.4 1.0 %copy-start = (f32[4,2,16,512]{3,2,1,0:T(8,128)S(1)}, f32[4,2,16,512]{3,2,1,0:T(8,128)}, u32[]{:S(2)}) copy-start(f32[4,2,16,512]{3,2,1,0:T(8,128)} %basis_ref.1) | copy-start | bytes 786436
  2.4 0.8 %copy-start.1 = (f32[4,32,128]{2,1,0:T(8,128)S(1)}, f32[4,32,128]{2,1,0:T(8,128)}, u32[]{:S(2)}) copy-start(f32[4,32,128]{2,1,0:T(8,128)} %interp_ref.1) | copy-start | bytes 196612
  3.2 0.7 %copy-start.2 = (f32[3,512]{1,0:T(4,128)S(1)}, f32[3,512]{1,0:T(4,128)}, u32[]{:S(2)}) copy-start(f32[3,512]{1,0:T(4,128)} %offsets_ref.1) | copy-start | bytes 18436

commit v4 on v3

--- a/solution.py
+++ b/solution.py
@@ -16,6 +16,9 @@
 SHIFT_SCALE = 0.02
 EPSILON = 1e-06
 HIGHEST = lax.Precision.HIGHEST
+GROUP = 8
+QUARTER = math.pi / 2.0
+UNIT = WAVENUMBER / QUARTER
 
 
 def split(values):
@@ -37,23 +40,23 @@
 
 
 def helmholtz_pair(sources, targets):
-    spread = SMOOTHING * SMOOTHING
+    spread = (SMOOTHING * UNIT) ** 2
     for axis_index in range(3):
         step = sources[:, axis_index : axis_index + 1] - targets[axis_index : axis_index + 1, :]
         spread = spread + step * step
     inverse = lax.rsqrt(spread)
-    angle = WAVENUMBER * (spread * inverse)
-    factor = inverse * (1.0 / (4.0 * math.pi))
-    turns = jnp.floor(angle * (2.0 / math.pi) + 0.5)
+    angle = spread * inverse
+    factor = inverse * (UNIT / (4.0 * math.pi))
+    turns = jnp.floor(angle + 0.5)
     quarter = turns.astype(jnp.int32)
-    rest = angle - turns * 1.5703125
-    rest = rest - turns * 4.837512969970703125e-4
-    rest = rest - turns * 7.54978995489188216e-8
+    rest = angle - turns
     square = rest * rest
-    sine = (-1.9515295891e-4 * square + 8.3321608736e-3) * square - 1.6666654611e-1
-    sine = sine * square * rest + rest
-    cosine = (2.443315711809948e-5 * square - 1.388731625493765e-3) * square
-    cosine = (cosine + 4.166664568298827e-2) * square * square - 0.5 * square + 1.0
+    sine = -1.9515295891e-4 * QUARTER**7 * square + 8.3321608736e-3 * QUARTER**5
+    sine = (sine * square - 1.6666654611e-1 * QUARTER**3) * square + QUARTER
+    sine = sine * rest
+    cosine = 2.443315711809948e-5 * QUARTER**8 * square - 1.388731625493765e-3 * QUARTER**6
+    cosine = (cosine * square + 4.166664568298827e-2 * QUARTER**4) * square - 0.5 * QUARTER**2
+    cosine = cosine * square + 1.0
     odd = (quarter & 1) == 1
     sine, cosine = jnp.where(odd, cosine, sine), jnp.where(odd, sine, cosine)
     sine_factor = jnp.where((quarter & 2) == 2, -factor, factor)
@@ -139,14 +142,23 @@
 
 def factor_rows(matrix, size):
     row_index = lax.broadcasted_iota(jnp.int32, matrix.shape, 0)
-    scale = jnp.zeros((size, 1), jnp.float32)
-    row_column = lax.broadcasted_iota(jnp.int32, (size, 1), 0)
-    for step in range(size):
-        pivot = matrix[step : step + 1, step : step + 1]
-        row = matrix[step : step + 1, :] * (1.0 / pivot)
-        column = matrix[:, step : step + 1]
-        scale = jnp.where(row_column == step, pivot, scale)
-        matrix = matrix - jnp.where(row_index > step, column * row, 0.0)
+    scale = jnp.ones_like(matrix)
+    for first in range(0, size, GROUP):
+        group = range(first, min(first + GROUP, size))
+        columns = [jnp.broadcast_to(matrix[:, j : j + 1], matrix.shape) for j in group]
+        rows = [matrix[j : j + 1, :] for j in group]
+        update = jnp.zeros_like(matrix)
+        for place, j in enumerate(group):
+            pivot = columns[place][j : j + 1, :]
+            inverse = 1.0 / pivot
+            scaled = rows[place] * inverse
+            scale = jnp.where(row_index == j, pivot, scale)
+            for other in range(place + 1, len(rows)):
+                entry = columns[place][first + other : first + other + 1, :]
+                rows[other] = rows[other] - entry * scaled
+                columns[other] = columns[other] - columns[place] * (entry * inverse)
+            update = update + jnp.where(row_index > j, columns[place] * scaled, 0.0)
+        matrix = matrix - update
     return matrix * lax.rsqrt(scale)
 
 
@@ -229,6 +241,7 @@
         ],
         axis=0,
     )
+    positions = positions * UNIT
     current = basis_ref[prior - 1].reshape(rows, local_points)
     sources = current * weights_ref[...]
     beside[1, :rows, :] = sources
@@ -275,7 +288,11 @@
     start_all("col", col_size, basis_source, basis_target, sems[0])
     own_box = lax.broadcasted_iota(jnp.int32, (box_count, 1), 0) + first_box
     slots = lax.broadcasted_iota(jnp.int32, near_boxes_ref.shape, 1)
-    distance = jnp.where(slots < near_count_ref[...], near_boxes_ref[...] - own_box, window)
+    count_index = lax.broadcasted_iota(jnp.int32, near_boxes_ref.shape, 0)
+    counts = jnp.zeros(near_boxes_ref.shape, jnp.int32)
+    for b in range(box_count):
+        counts = jnp.where(count_index == b, near_count_ref[b], counts)
+    distance = jnp.where(slots < counts, near_boxes_ref[...] - own_box, window)
     for o in range(window):
         times = jnp.sum((distance == o - reach).astype(jnp.float32), axis=1, keepdims=True)
         near_times[o] = jnp.broadcast_to(times, (box_count, box_points))
@@ -437,7 +454,7 @@
             jax.ShapeDtypeStruct((flat, all_columns), jnp.float32),
             jax.ShapeDtypeStruct(square, jnp.float32),
         ),
-        in_specs=[vmem] * 7,
+        in_specs=[vmem] * 6 + [pl.BlockSpec(memory_space=pltpu.SMEM)],
         out_specs=(vmem,) * 3,
         scratch_shapes=[pltpu.VMEM(shape, jnp.float32) for shape in shapes] + sems,
         compiler_params=pltpu.CompilerParams(
@@ -450,7 +467,7 @@
         interp,
         skeleton,
         near_boxes,
-        near_count.reshape(box_count, 1),
+        near_count,
     )
     coupling = coupling.reshape(prior, all_columns, all_columns)
     return block, coupling, factor[:, :all_columns]

time: 62.6 us -> 60.3 us (0.963)
  Pallas kernels: 55.7 us -> 51.5 us
  local copies, waits for them, and re-layouts: 5.15 us -> 7.08 us
    pallas_call x1, Pallas kernels: 55.7 us -> 51.5 us  [shards(): pl.pallas_call(functools.partial(step_kernel, box_size, col_size), out_sh...]
    unnamed x15 -> x17, local copies, waits for them, and re-layouts: 4.39 us -> 7.08 us
    reshape x1 -> x0, local copies, waits for them, and re-layouts: 0.76 us -> none  [shards(): near_count.reshape(box_count, 1)]
where the time goes in v4:
time: 60.3 us; the launch traced here: 59.2 us
  Pallas kernels  51.5 us (85%)
  local copies, waits for them, and re-layouts  7.08 us (12%)
  between operations  0.66 us (1%)
    pallas_call x1, Pallas kernels, shards(): pl.pallas_call(functools.partial(step_kernel, box_size, col_size), out_sh...  51.5 us
    unnamed x17, local copies, waits for them, and re-layouts  7.08 us

profile of v4, /device:TPU:0, one launch (start us, length us, event | category | flops | bytes accessed | tf_op | source)
XLA Modules:
  0.0 59.2 jit_solution(14863553466789285136)
XLA Ops:
  0.6 0.0 copy-start.6
  0.6 0.6 %copy-done.6 = s32[4]{0:T(128)S(1)} copy-done((s32[4]{0:T(128)S(1)}, s32[4]{0:T(128)}, u32[]{:S(2)}) %copy-start.6) | copy-done | bytes 40
  1.3 0.0 copy-start
  1.3 0.9 %copy-done = f32[4,2,16,512]{3,2,1,0:T(8,128)S(1)} copy-done((f32[4,2,16,512]{3,2,1,0:T(8,128)S(1)}, f32[4,2,16,512]{3,2,1,0:T(8,128)}, u32[]{:S(2)}) %copy-start) | copy-done | bytes 262168
  2.2 0.0 copy-start.1
  2.2 0.8 %copy-done.1 = f32[4,32,128]{2,1,0:T(8,128)S(1)} copy-done((f32[4,32,128]{2,1,0:T(8,128)S(1)}, f32[4,32,128]{2,1,0:T(8,128)}, u32[]{:S(2)}) %copy-start.1) | copy-done | bytes 65560
  3.1 0.0 copy-start.2
  3.1 0.7 %copy-done.2 = f32[3,512]{1,0:T(4,128)S(1)} copy-done((f32[3,512]{1,0:T(4,128)S(1)}, f32[3,512]{1,0:T(4,128)}, u32[]{:S(2)}) %copy-start.2) | copy-done | bytes 6168
  3.8 0.0 copy-start.3
  3.8 0.7 %copy-done.3 = f32[512]{0:T(512)S(1)} copy-done((f32[512]{0:T(512)S(1)}, f32[512]{0:T(512)}, u32[]{:S(2)}) %copy-start.3) | copy-done | bytes 2072
  4.5 0.0 copy-start.4
  4.5 0.7 %copy-done.4 = s32[4,32]{1,0:T(4,128)S(1)} copy-done((s32[4,32]{1,0:T(4,128)S(1)}, s32[4,32]{1,0:T(4,128)}, u32[]{:S(2)}) %copy-start.4) | copy-done | bytes 536
  5.1 0.0 copy-start.5
  5.1 0.7 %copy-done.5 = s32[4,27]{1,0:T(4,128)S(1)} copy-done((s32[4,27]{1,0:T(4,128)S(1)}, s32[4,27]{1,0:T(4,128)}, u32[]{:S(2)}) %copy-start.5) | copy-done | bytes 456
  5.8 51.5 %shard_map.94 = (f32[2,16,512]{2,1,0:T(8,128)S(1)}, f32[256,64]{1,0:T(8,128)S(1)}, f32[64,128]{1,0:T(8,128)S(1)}) custom-call(f32[4,2,16,512]{3,2,1,0:T(8,128)S(1)} %copy-done, f32[3,512]{1,0:T(4,128)S(1)} %copy-done.2, f32[1,512]{1,0:T(1,128)S(1)} %bitcast.5, f32[4,32,128]{2,1,0:T(8,128)S(1)} %copy-done.1, s32[4,32]{1,0:T(4,128)S(1)} %copy-done.4, ...), custom_call_target="tpu_custom_call" | custom-call | tf_op jit(solution)/shard_map/pallas_call | solution.py:450
  57.3 0.6 %copy.13 = f32[2,16,512]{2,1,0:T(8,128)} copy(f32[2,16,512]{2,1,0:T(8,128)S(1)} %get-tuple-element.12) | data formatting | bytes 131072
  57.9 0.7 %copy.14 = f32[4,64,64]{2,1,0:T(8,128)} copy(f32[4,64,64]{2,1,0:T(8,128)S(1)} %bitcast.3) | data formatting | bytes 131072
  58.6 0.6 %copy.15 = f32[64,64]{1,0:T(8,128)} copy(f32[64,64]{1,0:T(8,128)S(1)} %bitcast.4) | data formatting | bytes 32768
Async XLA Ops:
  0.6 0.7 %copy-start.6 = (s32[4]{0:T(128)S(1)}, s32[4]{0:T(128)}, u32[]{:S(2)}) copy-start(s32[4]{0:T(128)} %near_count_ref.1) | copy-start | bytes 52
  1.3 0.9 %copy-start = (f32[4,2,16,512]{3,2,1,0:T(8,128)S(1)}, f32[4,2,16,512]{3,2,1,0:T(8,128)}, u32[]{:S(2)}) copy-start(f32[4,2,16,512]{3,2,1,0:T(8,128)} %basis_ref.1) | copy-start | bytes 786436
  2.2 0.8 %copy-start.1 = (f32[4,32,128]{2,1,0:T(8,128)S(1)}, f32[4,32,128]{2,1,0:T(8,128)}, u32[]{:S(2)}) copy-start(f32[4,32,128]{2,1,0:T(8,128)} %interp_ref.1) | copy-start | bytes 196612
  3.1 0.7 %copy-start.2 = (f32[3,512]{1,0:T(4,128)S(1)}, f32[3,512]{1,0:T(4,128)}, u32[]{:S(2)}) copy-start(f32[3,512]{1,0:T(4,128)} %offsets_ref.1) | copy-start | bytes 18436
  3.8 0.7 %copy-start.3 = (f32[512]{0:T(512)S(1)}, f32[512]{0:T(512)}, u32[]{:S(2)}) copy-start(f32[512]{0:T(512)} %param.9) | copy-start | bytes 6148
  4.5 0.7 %copy-start.4 = (s32[4,32]{1,0:T(4,128)S(1)}, s32[4,32]{1,0:T(4,128)}, u32[]{:S(2)}) copy-start(s32[4,32]{1,0:T(4,128)} %skeleton_ref.1) | copy-start | bytes 1540
  5.1 0.7 %copy-start.5 = (s32[4,27]{1,0:T(4,128)S(1)}, s32[4,27]{1,0:T(4,128)}, u32[]{:S(2)}) copy-start(s32[4,27]{1,0:T(4,128)} %near_boxes_ref.1) | copy-start | bytes 1300

commit v5 on v4

--- a/solution.py
+++ b/solution.py
@@ -349,7 +349,6 @@
     start_all("col", col_size, applied_source, applied_target, sems[1])
     row_basis[:, :, rows_of(col, columns), :] = basis_ref[:, :, :, rows_of(col, points)]
     row_applied[:, rows_of(col, columns), :] = applied_ref[:, :, rows_of(col, points)]
-    wait_all("col", col_size, applied_source, applied_target, sems[1])
     wait_all("col", col_size, basis_source, basis_target, sems[0])
     flat_basis = jnp.concatenate(
         [
@@ -358,6 +357,7 @@
         ],
         axis=1,
     )
+    wait_all("col", col_size, applied_source, applied_target, sems[1])
     flat_applied = jnp.concatenate([row_applied[0], row_applied[1]], axis=1)
     part[...] = nt_dot(flat_applied, flat_basis) * (1.0 / row_total)
     col_parts[col] = part[rows_of(col, share), :]
@@ -458,7 +458,7 @@
         out_specs=(vmem,) * 3,
         scratch_shapes=[pltpu.VMEM(shape, jnp.float32) for shape in shapes] + sems,
         compiler_params=pltpu.CompilerParams(
-            collective_id=0, has_side_effects=True, vmem_limit_bytes=40 * 1024 * 1024
+            collective_id=0, has_side_effects=True, vmem_limit_bytes=63 * 1024 * 1024
         ),
     )(
         basis,

time: 60.3 us -> 57.2 us (0.949)
  local copies, waits for them, and re-layouts: 7.08 us -> 2.88 us
  Pallas kernels: 51.5 us -> 52.6 us
    unnamed x17 -> x7, local copies, waits for them, and re-layouts: 7.08 us -> 2.88 us
    pallas_call x1, Pallas kernels: 51.5 us -> 52.6 us  [shards(): pl.pallas_call(functools.partial(step_kernel, box_size, col_size), out_sh...]
where the time goes in v5:
time: 57.2 us; the launch traced here: 56.1 us
  Pallas kernels  52.6 us (92%)
  local copies, waits for them, and re-layouts  2.88 us (5%)
  between operations  0.65 us (1%)
    pallas_call x1, Pallas kernels, shards(): pl.pallas_call(functools.partial(step_kernel, box_size, col_size), out_sh...  52.6 us
    unnamed x7, local copies, waits for them, and re-layouts  2.88 us

profile of v5, /device:TPU:0, one launch (start us, length us, event | category | flops | bytes accessed | tf_op | source)
XLA Modules:
  0.0 56.1 jit_solution(1295741735393503828)
XLA Ops:
  0.6 52.6 %shard_map.94 = (f32[2,16,512]{2,1,0:T(8,128)}, f32[256,64]{1,0:T(8,128)}, f32[64,128]{1,0:T(8,128)}) custom-call(f32[4,2,16,512]{3,2,1,0:T(8,128)} %basis_ref.1, f32[3,512]{1,0:T(4,128)} %offsets_ref.1, f32[1,512]{1,0:T(1,128)} %bitcast.5, f32[4,32,128]{2,1,0:T(8,128)} %interp_ref.1, s32[4,32]{1,0:T(4,128)} %skeleton_ref.1, s32[4,27]{1,0:T(4,128)} %near_boxes_ref.1, ...), custom_call_target="tpu_custom_call" | custom-call | tf_op jit(solution)/shard_map/pallas_call | solution.py:450
  53.2 0.0 copy-start
  53.3 1.5 %copy.13 = f32[2,16,512]{2,1,0:T(8,128)} copy(f32[2,16,512]{2,1,0:T(8,128)} %get-tuple-element.12) | data formatting | bytes 131072
  54.8 0.0 copy-done
  54.8 0.0 copy-start.1
  54.8 0.7 %copy.14 = f32[4,64,64]{2,1,0:T(8,128)} copy(f32[4,64,64]{2,1,0:T(8,128)S(1)} %bitcast.3) | data formatting | bytes 131072
  55.4 0.1 copy-done.1
  55.5 0.6 %copy.15 = f32[64,64]{1,0:T(8,128)} copy(f32[64,64]{1,0:T(8,128)S(1)} %bitcast.4) | data formatting | bytes 32768
Async XLA Ops:
  53.2 1.5 %copy-start = (f32[256,64]{1,0:T(8,128)S(1)}, f32[256,64]{1,0:T(8,128)}, u32[]{:S(2)}) copy-start(f32[256,64]{1,0:T(8,128)} %get-tuple-element.7) | copy-start | bytes 196612
  54.8 0.8 %copy-start.1 = (f32[64,128]{1,0:T(8,128)S(1)}, f32[64,128]{1,0:T(8,128)}, u32[]{:S(2)}) copy-start(f32[64,128]{1,0:T(8,128)} %get-tuple-element.8) | copy-start | bytes 98308
